TPU v7x, 128 devices: a whole 4x4x4 slice. The times are simulated.
128 devices in a mesh: layer: 8 (over z, core), front: 16 (over y, x).
Axes of the slice: x: 4, y: 4, z: 4, core: 2. Of those that a mesh axis runs over, the one named last changes fastest.
Arguments:
- factor: bfloat16 [8, 2, 8192, 8192], P('layer', None, 'front'), may hold values from -0.046875 to 0.046875
- right_side: bfloat16 [8, 2, 8192, 256], P('layer', None, 'front'), may hold values from -6 to 6
- coupling: float32 [8, 8192], P('layer', 'front'), may hold values from 0.5 to 1.5
- forward: bfloat16 [8, 2, 8192, 256], P('layer', None, 'front'), may hold values from -6 to 6
Outputs:
- adjoint: bfloat16 [8, 2, 8192, 256], P('layer', None, 'front')
- gradient: float32 [8, 8192], P('layer', 'front')
All inputs are finite; a program needn't handle non-finite values.
Results may differ from a plain program's by a relative error of at most 0.019.
Values may be sent and summed in bfloat16 or wider, within the bound.
No kernel may reach another device: no remote copies, remote signals or barrier semaphores. Data moves between devices by JAX's collectives and lax.ppermute only.
A program may use at most 128 MiB of HBM per device.

v0:
```python
import math

import jax
import jax.numpy as jnp
from jax import lax
from jax.sharding import PartitionSpec as P


def from_behind(value, axis, steps):
    count = lax.axis_size(axis)
    leading, last = (max(0, -steps), min(count, count - steps))
    return lax.ppermute(value, axis, [(source, source + steps) for source in range(leading, last)])


def on_device(factor, right_side, coupling, forward):
    panels = factor[0]
    local_rhs = right_side[0]
    sources = local_rhs.shape[2]
    row_count = local_rhs.shape[1]
    block_count = 4
    width = sources // block_count
    depth = lax.axis_size("layer")
    position = lax.axis_index("layer")
    couple = coupling[0][None, :, None]

    def accumulate(piece):
        joined = jnp.concatenate((piece[0], piece[1]), axis=1)
        plain = jnp.dot(panels[0], joined, preferred_element_type=jnp.float32)
        twisted = jnp.dot(panels[1], joined, preferred_element_type=jnp.float32)
        return (plain[:, :width] - twisted[:, width:], plain[:, width:] + twisted[:, :width])

    def advance(counter, carry):
        result, upper = carry
        received = from_behind(upper, "layer", -1)
        block_index = counter - (depth - 1 - position)
        is_live = (block_index >= 0) & (block_index < block_count)
        start = jnp.clip(block_index, 0, block_count - 1) * width
        block_rhs = lax.dynamic_slice_in_dim(local_rhs, start, width, 2)
        merged = (block_rhs.astype(jnp.float32) + couple * received.astype(jnp.float32)).astype(
            jnp.bfloat16
        )
        real_part, imag_part = accumulate(lax.all_gather(merged, "front", axis=1, tiled=True))
        fresh = jnp.stack((real_part, imag_part)).astype(jnp.bfloat16)
        previous = lax.dynamic_slice_in_dim(result, start, width, 2)
        kept = jnp.where(is_live, fresh, previous)
        result = lax.dynamic_update_slice_in_dim(result, kept, start, 2)
        return (result, fresh)

    initial = (
        jnp.zeros((2, row_count, sources), jnp.bfloat16),
        jnp.zeros((2, row_count, width), jnp.bfloat16),
    )
    result, finished = lax.fori_loop(0, block_count + depth - 1, advance, initial)
    field_fwd = forward[0].astype(jnp.float32)
    field_adj = result.astype(jnp.float32)
    gradient = jnp.sum(
        field_fwd[0] * field_adj[0] - field_fwd[1] * field_adj[1], axis=-1
    ) / math.sqrt(sources)
    return (result[None], gradient[None])


def solution(mesh):
    placed = (
        P("layer", None, "front", None),
        P("layer", None, "front", None),
        P("layer", "front"),
        P("layer", None, "front", None),
    )
    return jax.shard_map(
        on_device,
        mesh=mesh,
        in_specs=placed,
        out_specs=(P("layer", None, "front", None), P("layer", "front")),
        check_vma=False,
    )
```

profile of v0, /device:TPU:1, one launch (start us, length us, event | category | flops | bytes accessed | tf_op | source)
XLA Modules:
  0.0 745.9 jit_solution(2174115341082282529)
XLA Ops:
  8.5 728.6 %while.17 = (s32[]{:T(128)}, bf16[2,512,256]{1,2,0:T(8,128)(2,1)S(1)}, bf16[2,512,64]{1,2,0:T(8,128)(2,1)S(1)}, s32[]{:T(128)}, bf16[2,512,256]{1,2,0:T(8,128)(2...) while((s32[]{:T(128)}, ...), condition=%wide.region_1.2_spmd, body=%wide.region_0.1_spmd.sunk | while | flops 2156658688 | bytes 101583200 | solution.py:53
  8.6 3.5 collective-permute-start
  12.0 4.2 collective-permute-done
  17.7 48.2 %all-gather.2.cloned.1.call-done = bf16[2,8192,64]{1,2,0:T(8,128)(2,1)} async-done(((bf16[2,512,64]{1,2,0:T(8,128)(2,1)}), bf16[2,8192,64]{1,2,0:T(8,128)(2,1)}) %all-gather.2.cloned.1.call-update) | async-done | bytes 2097168 | tf_op jit(solution)/shard_map/while/body/eval_jaxpr/all_gather | solution.py:42
  67.7 6.6 fusion.28
  77.8 3.4 collective-permute-start
  81.2 3.8 collective-permute-done
  86.4 45.4 %all-gather.2.cloned.1.call-done = bf16[2,8192,64]{1,2,0:T(8,128)(2,1)} async-done(((bf16[2,512,64]{1,2,0:T(8,128)(2,1)}), bf16[2,8192,64]{1,2,0:T(8,128)(2,1)}) %all-gather.2.cloned.1.call-update) | async-done | bytes 2097168 | tf_op jit(solution)/shard_map/while/body/eval_jaxpr/all_gather | solution.py:42
  133.7 6.6 fusion.28
  143.7 3.4 collective-permute-start
  147.2 3.8 collective-permute-done
  152.4 45.4 %all-gather.2.cloned.1.call-done = bf16[2,8192,64]{1,2,0:T(8,128)(2,1)} async-done(((bf16[2,512,64]{1,2,0:T(8,128)(2,1)}), bf16[2,8192,64]{1,2,0:T(8,128)(2,1)}) %all-gather.2.cloned.1.call-update) | async-done | bytes 2097168 | tf_op jit(solution)/shard_map/while/body/eval_jaxpr/all_gather | solution.py:42
  199.6 6.6 fusion.28
  209.6 3.4 collective-permute-start
  213.1 3.8 collective-permute-done
  218.3 45.4 %all-gather.2.cloned.1.call-done = bf16[2,8192,64]{1,2,0:T(8,128)(2,1)} async-done(((bf16[2,512,64]{1,2,0:T(8,128)(2,1)}), bf16[2,8192,64]{1,2,0:T(8,128)(2,1)}) %all-gather.2.cloned.1.call-update) | async-done | bytes 2097168 | tf_op jit(solution)/shard_map/while/body/eval_jaxpr/all_gather | solution.py:42
  265.5 6.6 fusion.28
  272.5 2.9 fusion.27
  275.6 3.4 collective-permute-start
  279.0 3.8 collective-permute-done
  284.2 45.4 %all-gather.2.cloned.1.call-done = bf16[2,8192,64]{1,2,0:T(8,128)(2,1)} async-done(((bf16[2,512,64]{1,2,0:T(8,128)(2,1)}), bf16[2,8192,64]{1,2,0:T(8,128)(2,1)}) %all-gather.2.cloned.1.call-update) | async-done | bytes 2097168 | tf_op jit(solution)/shard_map/while/body/eval_jaxpr/all_gather | solution.py:42
  331.5 6.6 fusion.28
  338.4 2.9 fusion.27
  341.5 3.4 collective-permute-start
  345.0 3.8 collective-permute-done
  350.2 45.4 %all-gather.2.cloned.1.call-done = bf16[2,8192,64]{1,2,0:T(8,128)(2,1)} async-done(((bf16[2,512,64]{1,2,0:T(8,128)(2,1)}), bf16[2,8192,64]{1,2,0:T(8,128)(2,1)}) %all-gather.2.cloned.1.call-update) | async-done | bytes 2097168 | tf_op jit(solution)/shard_map/while/body/eval_jaxpr/all_gather | solution.py:42
  397.4 6.6 fusion.28
  404.4 2.9 fusion.27
  407.4 3.4 collective-permute-start
  410.9 3.8 collective-permute-done
  416.1 45.4 %all-gather.2.cloned.1.call-done = bf16[2,8192,64]{1,2,0:T(8,128)(2,1)} async-done(((bf16[2,512,64]{1,2,0:T(8,128)(2,1)}), bf16[2,8192,64]{1,2,0:T(8,128)(2,1)}) %all-gather.2.cloned.1.call-update) | async-done | bytes 2097168 | tf_op jit(solution)/shard_map/while/body/eval_jaxpr/all_gather | solution.py:42
  463.3 6.6 fusion.28
  473.4 3.4 collective-permute-start
  476.9 3.8 collective-permute-done
  482.0 45.4 %all-gather.2.cloned.1.call-done = bf16[2,8192,64]{1,2,0:T(8,128)(2,1)} async-done(((bf16[2,512,64]{1,2,0:T(8,128)(2,1)}), bf16[2,8192,64]{1,2,0:T(8,128)(2,1)}) %all-gather.2.cloned.1.call-update) | async-done | bytes 2097168 | tf_op jit(solution)/shard_map/while/body/eval_jaxpr/all_gather | solution.py:42
  529.3 6.6 fusion.28
  539.3 3.4 collective-permute-start
  542.8 3.8 collective-permute-done
  548.0 45.4 %all-gather.2.cloned.1.call-done = bf16[2,8192,64]{1,2,0:T(8,128)(2,1)} async-done(((bf16[2,512,64]{1,2,0:T(8,128)(2,1)}), bf16[2,8192,64]{1,2,0:T(8,128)(2,1)}) %all-gather.2.cloned.1.call-update) | async-done | bytes 2097168 | tf_op jit(solution)/shard_map/while/body/eval_jaxpr/all_gather | solution.py:42
  595.2 6.6 fusion.28
  605.3 3.4 collective-permute-start
  608.7 3.8 collective-permute-done
  613.9 45.4 %all-gather.2.cloned.1.call-done = bf16[2,8192,64]{1,2,0:T(8,128)(2,1)} async-done(((bf16[2,512,64]{1,2,0:T(8,128)(2,1)}), bf16[2,8192,64]{1,2,0:T(8,128)(2,1)}) %all-gather.2.cloned.1.call-update) | async-done | bytes 2097168 | tf_op jit(solution)/shard_map/while/body/eval_jaxpr/all_gather | solution.py:42
  661.2 6.6 fusion.28
  671.2 3.4 collective-permute-start
  674.7 3.8 collective-permute-done
  679.9 45.4 %all-gather.2.cloned.1.call-done = bf16[2,8192,64]{1,2,0:T(8,128)(2,1)} async-done(((bf16[2,512,64]{1,2,0:T(8,128)(2,1)}), bf16[2,8192,64]{1,2,0:T(8,128)(2,1)}) %all-gather.2.cloned.1.call-update) | async-done | bytes 2097168 | tf_op jit(solution)/shard_map/while/body/eval_jaxpr/all_gather | solution.py:42
  727.1 6.6 fusion.28
  (107 shorter events, 67.7 us)
Async XLA Ops:
  8.5 728.7 %copy-start = (bf16[1,2,512,256]{3,2,1,0:T(8,128)(2,1)S(1)}, bf16[1,2,512,256]{3,2,1,0:T(8,128)(2,1)}, u32[]{:S(2)}) copy-start(bf16[1,2,512,256]{3,2,1,0:T(8,128)(2,1)} %param.9) | copy-start | bytes 1572868
  8.5 57.4 %all-gather.2.cloned.1.call-start = ((), (), s32[]{:S(2)}) async-start(), calls=%async_computation | async-start | bytes 2228224 | tf_op jit(solution)/shard_map/while/body/eval_jaxpr/all_gather | solution.py:42
  8.6 7.7 %collective-permute-start = (bf16[2,512,64]{1,2,0:T(8,128)(2,1)S(1)}, bf16[2,512,64]{1,2,0:T(8,128)(2,1)S(1)}, u32[]{:S(2)}, u32[]{:S(2)}) collective-permute-start(bf16[2,512,64]{1,2,0:T(8,128)(2,1)S(1)} %get-tuple-element.263), channel_id=1, source_target_pairs={{16,0},{32,16},{48,32},{64,48},{80,64},{96,80},{112,96},{17,1},{33... | collective-permute-start | bytes 393224 | tf_op jit(solution)/shard_map/while/body/eval_jaxpr/ppermute | solution.py:12
  65.9 8.8 %copy-start.1 = (bf16[2,512,8192]{2,1,0:T(8,128)(2,1)S(1)}, bf16[2,512,8192]{2,1,0:T(8,128)(2,1)}, u32[]{:S(2)}) copy-start(bf16[2,512,8192]{2,1,0:T(8,128)(2,1)} %get-tuple-element.280) | copy-start | bytes 50331652 | tf_op jit(solution)/shard_map/while
  77.7 54.1 %all-gather.2.cloned.1.call-start = ((), (), s32[]{:S(2)}) async-start(), calls=%async_computation | async-start | bytes 2228224 | tf_op jit(solution)/shard_map/while/body/eval_jaxpr/all_gather | solution.py:42
  77.8 7.3 collective-permute-start
  131.8 8.8 %copy-start.1 = (bf16[2,512,8192]{2,1,0:T(8,128)(2,1)S(1)}, bf16[2,512,8192]{2,1,0:T(8,128)(2,1)}, u32[]{:S(2)}) copy-start(bf16[2,512,8192]{2,1,0:T(8,128)(2,1)} %get-tuple-element.280) | copy-start | bytes 50331652 | tf_op jit(solution)/shard_map/while
  143.7 54.1 %all-gather.2.cloned.1.call-start = ((), (), s32[]{:S(2)}) async-start(), calls=%async_computation | async-start | bytes 2228224 | tf_op jit(solution)/shard_map/while/body/eval_jaxpr/all_gather | solution.py:42
  143.7 7.3 collective-permute-start
  197.8 8.8 %copy-start.1 = (bf16[2,512,8192]{2,1,0:T(8,128)(2,1)S(1)}, bf16[2,512,8192]{2,1,0:T(8,128)(2,1)}, u32[]{:S(2)}) copy-start(bf16[2,512,8192]{2,1,0:T(8,128)(2,1)} %get-tuple-element.280) | copy-start | bytes 50331652 | tf_op jit(solution)/shard_map/while
  209.6 54.1 %all-gather.2.cloned.1.call-start = ((), (), s32[]{:S(2)}) async-start(), calls=%async_computation | async-start | bytes 2228224 | tf_op jit(solution)/shard_map/while/body/eval_jaxpr/all_gather | solution.py:42
  209.6 7.3 collective-permute-start
  263.7 8.8 %copy-start.1 = (bf16[2,512,8192]{2,1,0:T(8,128)(2,1)S(1)}, bf16[2,512,8192]{2,1,0:T(8,128)(2,1)}, u32[]{:S(2)}) copy-start(bf16[2,512,8192]{2,1,0:T(8,128)(2,1)} %get-tuple-element.280) | copy-start | bytes 50331652 | tf_op jit(solution)/shard_map/while
  275.5 54.1 %all-gather.2.cloned.1.call-start = ((), (), s32[]{:S(2)}) async-start(), calls=%async_computation | async-start | bytes 2228224 | tf_op jit(solution)/shard_map/while/body/eval_jaxpr/all_gather | solution.py:42
  275.6 7.3 collective-permute-start
  329.6 8.8 %copy-start.1 = (bf16[2,512,8192]{2,1,0:T(8,128)(2,1)S(1)}, bf16[2,512,8192]{2,1,0:T(8,128)(2,1)}, u32[]{:S(2)}) copy-start(bf16[2,512,8192]{2,1,0:T(8,128)(2,1)} %get-tuple-element.280) | copy-start | bytes 50331652 | tf_op jit(solution)/shard_map/while
  341.5 54.1 %all-gather.2.cloned.1.call-start = ((), (), s32[]{:S(2)}) async-start(), calls=%async_computation | async-start | bytes 2228224 | tf_op jit(solution)/shard_map/while/body/eval_jaxpr/all_gather | solution.py:42
  341.5 7.3 collective-permute-start
  395.6 8.8 %copy-start.1 = (bf16[2,512,8192]{2,1,0:T(8,128)(2,1)S(1)}, bf16[2,512,8192]{2,1,0:T(8,128)(2,1)}, u32[]{:S(2)}) copy-start(bf16[2,512,8192]{2,1,0:T(8,128)(2,1)} %get-tuple-element.280) | copy-start | bytes 50331652 | tf_op jit(solution)/shard_map/while
  407.4 54.1 %all-gather.2.cloned.1.call-start = ((), (), s32[]{:S(2)}) async-start(), calls=%async_computation | async-start | bytes 2228224 | tf_op jit(solution)/shard_map/while/body/eval_jaxpr/all_gather | solution.py:42
  407.4 7.3 collective-permute-start
  461.5 8.8 %copy-start.1 = (bf16[2,512,8192]{2,1,0:T(8,128)(2,1)S(1)}, bf16[2,512,8192]{2,1,0:T(8,128)(2,1)}, u32[]{:S(2)}) copy-start(bf16[2,512,8192]{2,1,0:T(8,128)(2,1)} %get-tuple-element.280) | copy-start | bytes 50331652 | tf_op jit(solution)/shard_map/while
  473.3 54.1 %all-gather.2.cloned.1.call-start = ((), (), s32[]{:S(2)}) async-start(), calls=%async_computation | async-start | bytes 2228224 | tf_op jit(solution)/shard_map/while/body/eval_jaxpr/all_gather | solution.py:42
  473.4 7.3 collective-permute-start
  527.4 8.8 %copy-start.1 = (bf16[2,512,8192]{2,1,0:T(8,128)(2,1)S(1)}, bf16[2,512,8192]{2,1,0:T(8,128)(2,1)}, u32[]{:S(2)}) copy-start(bf16[2,512,8192]{2,1,0:T(8,128)(2,1)} %get-tuple-element.280) | copy-start | bytes 50331652 | tf_op jit(solution)/shard_map/while
  539.3 54.1 %all-gather.2.cloned.1.call-start = ((), (), s32[]{:S(2)}) async-start(), calls=%async_computation | async-start | bytes 2228224 | tf_op jit(solution)/shard_map/while/body/eval_jaxpr/all_gather | solution.py:42
  539.3 7.3 collective-permute-start
  593.4 8.8 %copy-start.1 = (bf16[2,512,8192]{2,1,0:T(8,128)(2,1)S(1)}, bf16[2,512,8192]{2,1,0:T(8,128)(2,1)}, u32[]{:S(2)}) copy-start(bf16[2,512,8192]{2,1,0:T(8,128)(2,1)} %get-tuple-element.280) | copy-start | bytes 50331652 | tf_op jit(solution)/shard_map/while
  605.2 54.1 %all-gather.2.cloned.1.call-start = ((), (), s32[]{:S(2)}) async-start(), calls=%async_computation | async-start | bytes 2228224 | tf_op jit(solution)/shard_map/while/body/eval_jaxpr/all_gather | solution.py:42
  605.3 7.3 collective-permute-start
  659.3 8.8 %copy-start.1 = (bf16[2,512,8192]{2,1,0:T(8,128)(2,1)S(1)}, bf16[2,512,8192]{2,1,0:T(8,128)(2,1)}, u32[]{:S(2)}) copy-start(bf16[2,512,8192]{2,1,0:T(8,128)(2,1)} %get-tuple-element.280) | copy-start | bytes 50331652 | tf_op jit(solution)/shard_map/while
  671.1 54.1 %all-gather.2.cloned.1.call-start = ((), (), s32[]{:S(2)}) async-start(), calls=%async_computation | async-start | bytes 2228224 | tf_op jit(solution)/shard_map/while/body/eval_jaxpr/all_gather | solution.py:42
  671.2 7.3 collective-permute-start
  725.3 8.8 %copy-start.1 = (bf16[2,512,8192]{2,1,0:T(8,128)(2,1)S(1)}, bf16[2,512,8192]{2,1,0:T(8,128)(2,1)}, u32[]{:S(2)}) copy-start(bf16[2,512,8192]{2,1,0:T(8,128)(2,1)} %get-tuple-element.280) | copy-start | bytes 50331652 | tf_op jit(solution)/shard_map/while
Sparse Core Ops, SparseCore 0:
  17.8 48.0 all-gather.1
  86.5 45.2 all-gather.1
  152.5 45.2 all-gather.1
  218.4 45.2 all-gather.1
  284.3 45.2 all-gather.1
  350.3 45.2 all-gather.1
  416.2 45.2 all-gather.1
  482.2 45.2 all-gather.1
  548.1 45.2 all-gather.1
  614.0 45.2 all-gather.1
  680.0 45.2 all-gather.1
where the time goes:
time: 747 us; the launch traced here: 746 us
  waiting for transfers between devices  544 us (73%)
  matrix products  105 us (14%)
  starting transfers between devices  38.4 us (5%)
  local copies, waits for them, and re-layouts  26.6 us (4%)
  other arithmetic  17.1 us (2%)
  between operations  13.8 us (2%)
    all_gather x11, waiting for transfers between devices, advance(): lax.all_gather(merged, 'front', axis=1, tiled=True)  502 us
    dot_general x11, matrix products, accumulate(): plain = jnp.dot(panels[0], joined, preferred_element_type=jnp.float32)  72.4 us
    ppermute x11, waiting for transfers between devices, from_behind(): lax.ppermute(value, axis, [(source, source + steps) for source in range(l...  42 us
    ppermute x11, starting transfers between devices, from_behind(): lax.ppermute(value, axis, [(source, source + steps) for source in range(l...  38 us
    dot_general x11, matrix products, accumulate(): twisted = jnp.dot(panels[1], joined, preferred_element_type=jnp.float32)  32.1 us
    squeeze x11, local copies, waits for them, and re-layouts, accumulate(): joined = jnp.concatenate((piece[0], piece[1]), axis=1)  20.1 us
    convert_element_type x11, other arithmetic, advance(): (block_rhs.astype(jnp.float32) + couple * received.astype(jnp.float32)).a...  15.2 us
  transfers between devices with their start and end apart: 22, of which 22 were waited for; matrix products, arithmetic and copies ran while one was open for 0% of the time, Pallas kernels for 0%

commit v1 on v0

v1 whole, which is shorter than its diff:
```python
import math

import jax
import jax.numpy as jnp
from jax import lax
from jax.experimental import pallas as pl
from jax.experimental.pallas import tpu as pltpu
from jax.sharding import PartitionSpec as P

AXES = ("layer", "front")
BLOCKS = 4
SIDE = 4
IN_VMEM = pl.BlockSpec(memory_space=pltpu.VMEM)
IN_SMEM = pl.BlockSpec(memory_space=pltpu.SMEM)
IN_HBM = pl.BlockSpec(memory_space=pltpu.HBM)


def arrange(factor, order):
    rows, columns = factor.shape
    fronts = order.shape[0]
    width = columns // fronts

    def body(order_ref, source, target, sem):
        def copy(i):
            start = pl.multiple_of(order_ref[i] * width, width)
            return pltpu.make_async_copy(
                source.at[:, pl.ds(start, width)], target.at[:, pl.ds(i * width, width)], sem.at[i]
            )

        for i in range(fronts):
            copy(i).start()
        for i in range(fronts):
            copy(i).wait()

    return pl.pallas_call(
        body,
        in_specs=[IN_SMEM, IN_HBM],
        out_specs=IN_VMEM,
        out_shape=pltpu.VMEM((rows, columns), factor.dtype),
        scratch_shapes=[pltpu.SemaphoreType.DMA((fronts,))],
        compiler_params=pltpu.CompilerParams(vmem_limit_bytes=32 << 20),
        cost_estimate=pl.CostEstimate(flops=0, bytes_accessed=2 * rows * columns, transcendentals=0),
        name="arrange",
    )(order, factor)


def term(panel_ref, group, pieces):
    span = panel_ref.shape[1] // SIDE
    joined = jnp.concatenate([pieces[i] for i in range(SIDE)], axis=1)
    return lax.dot_general(
        panel_ref[:, group * span:(group + 1) * span],
        joined,
        (((1,), (1,)), ((), ())),
        preferred_element_type=jnp.float32,
    )


def start_product(panel, near):
    rows, columns = panel.shape
    height = near.shape[1]

    def body(panel_ref, near_ref, total_ref):
        total_ref[...] = term(panel_ref, 0, near_ref)

    return pl.pallas_call(
        body,
        in_specs=[IN_VMEM] * 2,
        out_specs=IN_VMEM,
        out_shape=jax.ShapeDtypeStruct((rows, height), jnp.float32),
        compiler_params=pltpu.CompilerParams(vmem_limit_bytes=16 << 20),
        cost_estimate=pl.CostEstimate(
            flops=rows * columns * height // 2, bytes_accessed=rows * columns // 2, transcendentals=0
        ),
        name="start_product",
    )(pltpu.with_memory_space_constraint(panel, pltpu.VMEM), near)


def finish_product(panel, total, groups, rhs, couple):
    rows, columns = panel.shape
    height = total.shape[1]
    half, middle = height // 2, rows // 2

    def body(panel_ref, total_ref, *refs):
        groups_refs = refs[:SIDE - 1]
        rhs_ref, couple_ref, field_ref, merged_ref, sum_ref = refs[SIDE - 1:]
        sum_ref[...] = total_ref[...]
        for i, group_ref in enumerate(groups_refs):
            sum_ref[...] += term(panel_ref, i + 1, group_ref)
        plain = sum_ref[:middle].T
        twisted = sum_ref[middle:].T
        field = jnp.concatenate(
            (plain[:half] - twisted[half:], plain[half:] + twisted[:half]), axis=0
        ).astype(field_ref.dtype)
        field_ref[...] = field
        merged = rhs_ref[...].astype(jnp.float32) + couple_ref[...] * field.astype(jnp.float32)
        merged_ref[...] = merged.astype(merged_ref.dtype)

    shape = jax.ShapeDtypeStruct((height, middle), jnp.bfloat16)
    return pl.pallas_call(
        body,
        in_specs=[IN_VMEM] * (SIDE + 3),
        out_specs=(IN_VMEM, IN_VMEM),
        out_shape=(shape, shape),
        scratch_shapes=[pltpu.VMEM((rows, height), jnp.float32)],
        compiler_params=pltpu.CompilerParams(vmem_limit_bytes=16 << 20),
        cost_estimate=pl.CostEstimate(
            flops=rows * columns * height * 3 // 2, bytes_accessed=rows * columns * 3 // 2, transcendentals=0
        ),
        name="finish_product",
    )(pltpu.with_memory_space_constraint(panel, pltpu.VMEM), total, *groups, rhs, couple)


def on_device(factor, right_side, coupling, forward):
    layers, fronts = lax.axis_size("layer"), lax.axis_size("front")
    position = lax.axis_index("layer")
    place = lax.axis_index("front")
    rows, sources = right_side.shape[2:]
    count = BLOCKS
    block = sources // count
    steps = count + layers - 1

    def device(layer, slow, fast):
        return layer % layers * fronts + slow % SIDE * SIDE + fast % SIDE

    def moves(down, near, far):
        pairs = []
        for layer in range(layers):
            reached = (layer - down) % layers
            slow_step, fast_step = (far, near) if reached % 2 == 0 else (near, far)
            for slow in range(SIDE):
                for fast in range(SIDE):
                    pairs.append(
                        (device(layer, slow, fast), device(reached, slow + slow_step, fast + fast_step))
                    )
        return pairs

    def moved(value, down, near, far):
        return lax.ppermute(value, AXES, moves(down, near, far))

    slow, fast = place // SIDE, place % SIDE
    even = position % 2 == 0
    order = []
    for far in range(SIDE):
        for near in range(SIDE):
            slow_step = jnp.where(even, far, near)
            fast_step = jnp.where(even, near, far)
            order.append((slow - slow_step) % SIDE * SIDE + (fast - fast_step) % SIDE)
    order = jnp.stack(order).astype(jnp.int32)
    panel = arrange(factor[0].reshape(2 * rows, -1), order)

    turned = jnp.swapaxes(right_side[0], 1, 2)
    blocks = turned.reshape(2, count, block, rows).swapaxes(0, 1).reshape(count, 2 * block, rows)

    up = [(l * fronts + f, (l + 1) % layers * fronts + f) for l in range(layers) for f in range(fronts)]
    next_rhs = lax.ppermute(blocks, AXES, up)
    next_couple = jnp.where(position == 0, 0.0, lax.ppermute(coupling, AXES, up))
    depth = jnp.where(position == 0, layers, position)
    next_rhs = jnp.pad(next_rhs, ((layers - 2, layers - 1), (0, 0), (0, 0)))
    next_rhs = lax.dynamic_slice_in_dim(next_rhs, depth - 1, steps - 1, 0)

    fields = []
    merged = blocks[0]
    for step in range(steps):
        down = min(step, 1)
        near = jnp.stack([merged if down == 0 and i == 0 else moved(merged, down, i, 0) for i in range(SIDE)])
        far = [moved(near, 0, 0, i) for i in range(1, SIDE)]
        total = start_product(panel, near)
        rhs = next_rhs[min(step, steps - 2)]
        field, merged = finish_product(panel, total, far, rhs, next_couple)
        fields.append(field)

    result = lax.dynamic_slice_in_dim(jnp.stack(fields), layers - 1 - position, count, 0)
    result = result.reshape(count, 2, block, rows).swapaxes(0, 1).reshape(2, sources, rows)
    result = jnp.swapaxes(result, 1, 2)
    field_fwd = forward[0].astype(jnp.float32)
    field_adj = result.astype(jnp.float32)
    gradient = jnp.sum(
        field_fwd[0] * field_adj[0] - field_fwd[1] * field_adj[1], axis=-1
    ) / math.sqrt(sources)
    return (result[None], gradient[None])


def solution(mesh):
    placed = (
        P("layer", None, "front", None),
        P("layer", None, "front", None),
        P("layer", "front"),
        P("layer", None, "front", None),
    )
    return jax.shard_map(
        on_device,
        mesh=mesh,
        in_specs=placed,
        out_specs=(P("layer", None, "front", None), P("layer", "front")),
        check_vma=False,
    )
```

time: 747 us -> 356 us (0.48)
  waiting for transfers between devices: 544 us -> 164 us
  matrix products: 105 us -> 0 us
  starting transfers between devices: 38.4 us -> 113 us
  Pallas kernels: 0 us -> 55 us
  local copies, waits for them, and re-layouts: 26.6 us -> 8.84 us
  between operations: 13.8 us -> 1.55 us
  other arithmetic: 17.1 us -> 7.01 us
    all_gather x11 -> x0, waiting for transfers between devices: 502 us -> none  [advance(): lax.all_gather(merged, 'front', axis=1, tiled=True)]
    ppermute x11 -> x78, waiting for transfers between devices: 42 us -> 164 us  [the longest x76 164 us: moved(): return lax.ppermute(value, AXES, moves(down, near, far))]
    dot_general x22 -> x0, matrix products: 105 us -> none  [the longest x11 72.4 us: accumulate(): plain = jnp.dot(panels[0], joined, preferred_element_type=jnp.float32)]
    ppermute x11 -> x78, starting transfers between devices: 38 us -> 113 us  [the longest x76 106 us: moved(): return lax.ppermute(value, AXES, moves(down, near, far))]
    pallas_call x0 -> x22, Pallas kernels: none -> 55 us  [the longest x10 34.7 us: finish_product(): pl.pallas_call(body, in_specs=[IN_VMEM] * (SIDE + 3), out_specs=(IN_VMEM,...]
    squeeze x11 -> x2, local copies, waits for them, and re-layouts: 20.1 us -> 0.28 us  [on_device(): rhs = next_rhs[min(step, steps - 2)]]
    convert_element_type x11 -> x0, other arithmetic: 15.2 us -> none  [advance(): (block_rhs.astype(jnp.float32) + couple * received.astype(jnp.float32)).a...]
  transfers between devices with their start and end apart: 22 -> 78, of which waited for: 22 -> 60; matrix products, arithmetic and copies ran while one was open for 0% -> 0% of each run, Pallas kernels for 0% -> 6%
where the time goes in v1:
time: 356 us; the launch traced here: 349 us
  waiting for transfers between devices  164 us (46%)
  starting transfers between devices  113 us (32%)
  Pallas kernels  55 us (15%)
  local copies, waits for them, and re-layouts  8.84 us (2%)
  other arithmetic  7.01 us (2%)
    ppermute x76, waiting for transfers between devices, moved(): return lax.ppermute(value, AXES, moves(down, near, far))  164 us
    ppermute x76, starting transfers between devices, moved(): return lax.ppermute(value, AXES, moves(down, near, far))  106 us
    pallas_call x10, Pallas kernels, finish_product(): pl.pallas_call(body, in_specs=[IN_VMEM] * (SIDE + 3), out_specs=(IN_VMEM,...  34.7 us
    pallas_call x11, Pallas kernels, start_product(): pl.pallas_call(body, in_specs=[IN_VMEM] * 2, out_specs=IN_VMEM, out_shape...  13.7 us
    unnamed x21, local copies, waits for them, and re-layouts  8.35 us
  transfers between devices with their start and end apart: 78, of which 60 were waited for; matrix products, arithmetic and copies ran while one was open for 0% of the time, Pallas kernels for 6%

profile of v1, /device:TPU:1, one launch (start us, length us, event | category | flops | bytes accessed | tf_op | source)
XLA Modules:
  0.0 349.3 jit_solution(4190919536953088276)
XLA Ops:
  1.9 3.6 %collective-permute-start.2 = (bf16[128,512]{1,0:T(8,128)(2,1)S(1)}, bf16[128,512]{1,0:T(8,128)(2,1)S(1)}, u32[]{:S(2)}, u32[]{:S(2)}) collective-permute-start(bf16[128,512]{1,0:T(8,128)(2,1)S(1)} %bitcast.137), channel_id=1, source_target_pairs={{0,3},{1,0},{2,1},{3,2},{4,7},{5,4},{6,5},{7,6},{8,11},{9,8},{10,9... | collective-permute-start | bytes 393224 | tf_op jit(solution)/shard_map/ppermute | solution.py:138
  17.5 4.1 %collective-permute-start.7 = (f32[1,512]{1,0:T(1,128)S(1)}, f32[1,512]{1,0:T(1,128)S(1)}, u32[]{:S(2)}, u32[]{:S(2)}) collective-permute-start(f32[1,512]{1,0:T(1,128)S(1)} %copy-done.3), channel_id=1, source_target_pairs={{0,16},{1,17},{2,18},{3,19},{4,20},{5,21},{6,22},{7,23},{8,24},{9,... | collective-permute-start | bytes 6152 | tf_op jit(solution)/shard_map/ppermute | solution.py:156
  21.7 6.6 %arrange.1.panel_ref = bf16[1024,8192]{1,0:T(8,128)(2,1)S(1)} custom-call(s32[16]{0:T(128)S(1)} %stack.265.order_ref, bf16[1024,8192]{1,0:T(8,128)(2,1)} %bitcast.131), custom_call_target="tpu_custom_call" | custom-call | bytes 16777216 | tf_op jit(solution)/shard_map/arrange/pallas_call | solution.py:35
  29.9 3.5 finish_product.11
  35.2 3.6 %collective-permute-start.10 = (bf16[128,512]{1,0:T(8,128)(2,1)S(1)}, bf16[128,512]{1,0:T(8,128)(2,1)S(1)}, u32[]{:S(2)}, u32[]{:S(2)}) collective-permute-start(bf16[128,512]{1,0:T(8,128)(2,1)S(1)} %get-tuple-element.24), channel_id=1, source_target_pairs={{0,120},{1,121},{2,122},{3,123},{4,124},{5,125},{6,126},{7,127},{8... | collective-permute-start | bytes 393224 | tf_op jit(solution)/shard_map/ppermute | solution.py:138
  38.8 3.9 %collective-permute-start.9 = (bf16[128,512]{1,0:T(8,128)(2,1)S(1)}, bf16[128,512]{1,0:T(8,128)(2,1)S(1)}, u32[]{:S(2)}, u32[]{:S(2)}) collective-permute-start(bf16[128,512]{1,0:T(8,128)(2,1)S(1)} %get-tuple-element.24), channel_id=1, source_target_pairs={{0,116},{1,117},{2,118},{3,119},{4,120},{5,121},{6,122},{7,123},{8... | collective-permute-start | bytes 393224 | tf_op jit(solution)/shard_map/ppermute | solution.py:138
  51.4 5.4 %collective-permute-done.12.refs_0_ = bf16[4,128,512]{2,1,0:T(8,128)(2,1)S(1)} collective-permute-done((bf16[4,128,512]{2,1,0:T(8,128)(2,1)S(1)}, bf16[4,128,512]{2,1,0:T(8,128)(2,1)S(1)}, u32[]{:S(2)}, u32[]{:S(2)}) %collective-permute-start.12) | collective-permute-done | bytes 524320 | tf_op jit(solution)/shard_map/ppermute | solution.py:138
  56.8 5.6 %collective-permute-done.13.refs_1_ = bf16[4,128,512]{2,1,0:T(8,128)(2,1)S(1)} collective-permute-done((bf16[4,128,512]{2,1,0:T(8,128)(2,1)S(1)}, bf16[4,128,512]{2,1,0:T(8,128)(2,1)S(1)}, u32[]{:S(2)}, u32[]{:S(2)}) %collective-permute-start.13) | collective-permute-done | bytes 524320 | tf_op jit(solution)/shard_map/ppermute | solution.py:138
  63.1 3.5 finish_product.12
  68.1 3.6 %collective-permute-start.17 = (bf16[128,512]{1,0:T(8,128)(2,1)S(1)}, bf16[128,512]{1,0:T(8,128)(2,1)S(1)}, u32[]{:S(2)}, u32[]{:S(2)}) collective-permute-start(bf16[128,512]{1,0:T(8,128)(2,1)S(1)} %get-tuple-element.26), channel_id=1, source_target_pairs={{0,120},{1,121},{2,122},{3,123},{4,124},{5,125},{6,126},{7,127},{8... | collective-permute-start | bytes 393224 | tf_op jit(solution)/shard_map/ppermute | solution.py:138
  71.9 3.0 collective-permute-done.17
  74.9 3.2 collective-permute-done.16
  84.0 3.9 %collective-permute-done.19.refs_0_ = bf16[4,128,512]{2,1,0:T(8,128)(2,1)S(1)} collective-permute-done((bf16[4,128,512]{2,1,0:T(8,128)(2,1)S(1)}, bf16[4,128,512]{2,1,0:T(8,128)(2,1)S(1)}, u32[]{:S(2)}, u32[]{:S(2)}) %collective-permute-start.19) | collective-permute-done | bytes 524320 | tf_op jit(solution)/shard_map/ppermute | solution.py:138
  87.8 5.9 %collective-permute-done.20.refs_1_ = bf16[4,128,512]{2,1,0:T(8,128)(2,1)S(1)} collective-permute-done((bf16[4,128,512]{2,1,0:T(8,128)(2,1)S(1)}, bf16[4,128,512]{2,1,0:T(8,128)(2,1)S(1)}, u32[]{:S(2)}, u32[]{:S(2)}) %collective-permute-start.20) | collective-permute-done | bytes 524320 | tf_op jit(solution)/shard_map/ppermute | solution.py:138
  94.1 3.5 finish_product.13
  102.9 4.2 %collective-permute-done.24 = bf16[128,512]{1,0:T(8,128)(2,1)S(1)} collective-permute-done((bf16[128,512]{1,0:T(8,128)(2,1)S(1)}, bf16[128,512]{1,0:T(8,128)(2,1)S(1)}, u32[]{:S(2)}, u32[]{:S(2)}) %collective-permute-start.24) | collective-permute-done | bytes 131104 | tf_op jit(solution)/shard_map/ppermute | solution.py:138
  115.4 9.4 %collective-permute-done.26.refs_0_ = bf16[4,128,512]{2,1,0:T(8,128)(2,1)S(1)} collective-permute-done((bf16[4,128,512]{2,1,0:T(8,128)(2,1)S(1)}, bf16[4,128,512]{2,1,0:T(8,128)(2,1)S(1)}, u32[]{:S(2)}, u32[]{:S(2)}) %collective-permute-start.26) | collective-permute-done | bytes 524320 | tf_op jit(solution)/shard_map/ppermute | solution.py:138
  125.6 3.5 finish_product.14
  130.6 3.1 collective-permute-start.31
  145.6 4.2 %collective-permute-done.33.refs_0_ = bf16[4,128,512]{2,1,0:T(8,128)(2,1)S(1)} collective-permute-done((bf16[4,128,512]{2,1,0:T(8,128)(2,1)S(1)}, bf16[4,128,512]{2,1,0:T(8,128)(2,1)S(1)}, u32[]{:S(2)}, u32[]{:S(2)}) %collective-permute-start.33) | collective-permute-done | bytes 524320 | tf_op jit(solution)/shard_map/ppermute | solution.py:138
  149.9 5.9 %collective-permute-done.34.refs_1_ = bf16[4,128,512]{2,1,0:T(8,128)(2,1)S(1)} collective-permute-done((bf16[4,128,512]{2,1,0:T(8,128)(2,1)S(1)}, bf16[4,128,512]{2,1,0:T(8,128)(2,1)S(1)}, u32[]{:S(2)}, u32[]{:S(2)}) %collective-permute-start.34) | collective-permute-done | bytes 524320 | tf_op jit(solution)/shard_map/ppermute | solution.py:138
  156.2 3.5 finish_product.15
  161.2 3.3 collective-permute-start.38
  176.8 3.7 %collective-permute-done.40.refs_0_ = bf16[4,128,512]{2,1,0:T(8,128)(2,1)S(1)} collective-permute-done((bf16[4,128,512]{2,1,0:T(8,128)(2,1)S(1)}, bf16[4,128,512]{2,1,0:T(8,128)(2,1)S(1)}, u32[]{:S(2)}, u32[]{:S(2)}) %collective-permute-start.40) | collective-permute-done | bytes 524320 | tf_op jit(solution)/shard_map/ppermute | solution.py:138
  180.6 5.9 %collective-permute-done.41.refs_1_ = bf16[4,128,512]{2,1,0:T(8,128)(2,1)S(1)} collective-permute-done((bf16[4,128,512]{2,1,0:T(8,128)(2,1)S(1)}, bf16[4,128,512]{2,1,0:T(8,128)(2,1)S(1)}, u32[]{:S(2)}, u32[]{:S(2)}) %collective-permute-start.41) | collective-permute-done | bytes 524320 | tf_op jit(solution)/shard_map/ppermute | solution.py:138
  186.8 3.5 finish_product.16
  195.7 3.5 collective-permute-done.45
  207.7 3.9 %collective-permute-done.47.refs_0_ = bf16[4,128,512]{2,1,0:T(8,128)(2,1)S(1)} collective-permute-done((bf16[4,128,512]{2,1,0:T(8,128)(2,1)S(1)}, bf16[4,128,512]{2,1,0:T(8,128)(2,1)S(1)}, u32[]{:S(2)}, u32[]{:S(2)}) %collective-permute-start.47) | collective-permute-done | bytes 524320 | tf_op jit(solution)/shard_map/ppermute | solution.py:138
  211.5 5.6 %collective-permute-done.48.refs_1_ = bf16[4,128,512]{2,1,0:T(8,128)(2,1)S(1)} collective-permute-done((bf16[4,128,512]{2,1,0:T(8,128)(2,1)S(1)}, bf16[4,128,512]{2,1,0:T(8,128)(2,1)S(1)}, u32[]{:S(2)}, u32[]{:S(2)}) %collective-permute-start.48) | collective-permute-done | bytes 524320 | tf_op jit(solution)/shard_map/ppermute | solution.py:138
  217.8 3.5 finish_product.17
  226.6 3.5 collective-permute-done.52
  238.8 3.7 %collective-permute-done.54.refs_0_ = bf16[4,128,512]{2,1,0:T(8,128)(2,1)S(1)} collective-permute-done((bf16[4,128,512]{2,1,0:T(8,128)(2,1)S(1)}, bf16[4,128,512]{2,1,0:T(8,128)(2,1)S(1)}, u32[]{:S(2)}, u32[]{:S(2)}) %collective-permute-start.54) | collective-permute-done | bytes 524320 | tf_op jit(solution)/shard_map/ppermute | solution.py:138
  242.5 5.8 %collective-permute-done.55.refs_1_ = bf16[4,128,512]{2,1,0:T(8,128)(2,1)S(1)} collective-permute-done((bf16[4,128,512]{2,1,0:T(8,128)(2,1)S(1)}, bf16[4,128,512]{2,1,0:T(8,128)(2,1)S(1)}, u32[]{:S(2)}, u32[]{:S(2)}) %collective-permute-start.55) | collective-permute-done | bytes 524320 | tf_op jit(solution)/shard_map/ppermute | solution.py:138
  248.7 3.5 finish_product.18
  257.7 3.7 %collective-permute-done.59 = bf16[128,512]{1,0:T(8,128)(2,1)} collective-permute-done((bf16[128,512]{1,0:T(8,128)(2,1)S(1)}, bf16[128,512]{1,0:T(8,128)(2,1)}, u32[]{:S(2)}, u32[]{:S(2)}) %collective-permute-start.59) | collective-permute-done | bytes 131104 | tf_op jit(solution)/shard_map/ppermute | solution.py:138
  269.5 5.8 %copy-done.1 = bf16[1024,8192]{1,0:T(8,128)(2,1)S(1)} copy-done((bf16[1024,8192]{1,0:T(8,128)(2,1)S(1)}, bf16[1024,8192]{1,0:T(8,128)(2,1)}, u32[]{:S(2)}) %copy-start.1) | copy-done | bytes 16777240
  276.5 3.9 %collective-permute-done.62.refs_1_ = bf16[4,128,512]{2,1,0:T(8,128)(2,1)S(1)} collective-permute-done((bf16[4,128,512]{2,1,0:T(8,128)(2,1)S(1)}, bf16[4,128,512]{2,1,0:T(8,128)(2,1)S(1)}, u32[]{:S(2)}, u32[]{:S(2)}) %collective-permute-start.62) | collective-permute-done | bytes 524320 | tf_op jit(solution)/shard_map/ppermute | solution.py:138
  281.0 3.5 finish_product.19
  286.2 3.3 collective-permute-start.66
  289.8 3.2 collective-permute-done.66
  293.0 3.0 collective-permute-done.65
  301.7 4.0 %collective-permute-done.68.refs_0_ = bf16[4,128,512]{2,1,0:T(8,128)(2,1)S(1)} collective-permute-done((bf16[4,128,512]{2,1,0:T(8,128)(2,1)S(1)}, bf16[4,128,512]{2,1,0:T(8,128)(2,1)S(1)}, u32[]{:S(2)}, u32[]{:S(2)}) %collective-permute-start.68) | collective-permute-done | bytes 524320 | tf_op jit(solution)/shard_map/ppermute | solution.py:138
  305.6 5.7 %collective-permute-done.69.refs_1_ = bf16[4,128,512]{2,1,0:T(8,128)(2,1)S(1)} collective-permute-done((bf16[4,128,512]{2,1,0:T(8,128)(2,1)S(1)}, bf16[4,128,512]{2,1,0:T(8,128)(2,1)S(1)}, u32[]{:S(2)}, u32[]{:S(2)}) %collective-permute-start.69) | collective-permute-done | bytes 524320 | tf_op jit(solution)/shard_map/ppermute | solution.py:138
  311.9 3.5 finish_product.20
  316.9 3.3 collective-permute-start.73
  332.3 4.1 %collective-permute-done.75 = bf16[4,128,512]{2,1,0:T(8,128)(2,1)S(1)} collective-permute-done((bf16[4,128,512]{2,1,0:T(8,128)(2,1)S(1)}, bf16[4,128,512]{2,1,0:T(8,128)(2,1)S(1)}, u32[]{:S(2)}, u32[]{:S(2)}) %collective-permute-start.75) | collective-permute-done | bytes 524320 | tf_op jit(solution)/shard_map/ppermute | solution.py:138
  336.4 5.8 %collective-permute-done.76 = bf16[4,128,512]{2,1,0:T(8,128)(2,1)S(1)} collective-permute-done((bf16[4,128,512]{2,1,0:T(8,128)(2,1)S(1)}, bf16[4,128,512]{2,1,0:T(8,128)(2,1)S(1)}, u32[]{:S(2)}, u32[]{:S(2)}) %collective-permute-start.76) | collective-permute-done | bytes 524320 | tf_op jit(solution)/shard_map/ppermute | solution.py:138
  342.7 4.1 %finish_product.21 = (bf16[11,128,512]{2,1,0:T(8,128)(2,1)S(1)}, bf16[128,512]{1,0:T(8,128)(2,1)}) fusion(bf16[11,128,512]{2,1,0:T(8,128)(2,1)S(1)} %bitcast_dynamic-update-slice_fusion.1, bf16[1024,8192]{1,0:T(8,128)(2,1)S(1)} %copy-done.1, f32[1024,128]{1,0:T(8,128)S(1)} %start_product.21, bf16[4,128,512]{2,1,0:T(8,128)(2,1)S(1)} %collective-permute-done.75, ...), kind=kCustom, calls=%fused_computation.28 | custom fusion | flops 1610612736 | bytes 19269632 | tf_op jit(solution)/shard_map/finish_product/pallas_call | solution.py:99
  (175 shorter events, 145.2 us)
Async XLA Ops:
  1.9 7.6 %collective-permute-start.2 = (bf16[128,512]{1,0:T(8,128)(2,1)S(1)}, bf16[128,512]{1,0:T(8,128)(2,1)S(1)}, u32[]{:S(2)}, u32[]{:S(2)}) collective-permute-start(bf16[128,512]{1,0:T(8,128)(2,1)S(1)} %bitcast.137), channel_id=1, source_target_pairs={{0,3},{1,0},{2,1},{3,2},{4,7},{5,4},{6,5},{7,6},{8,11},{9,8},{10,9... | collective-permute-start | bytes 393224 | tf_op jit(solution)/shard_map/ppermute | solution.py:138
  6.6 23.0 %collective-permute-start.6 = (bf16[4,128,512]{2,1,0:T(8,128)(2,1)S(1)}, bf16[4,128,512]{2,1,0:T(8,128)(2,1)S(1)}, u32[]{:S(2)}, u32[]{:S(2)}) collective-permute-start(bf16[4,128,512]{2,1,0:T(8,128)(2,1)S(1)} %bitcast.136), channel_id=1, source_target_pairs={{0,16},{1,17},{2,18},{3,19},{4,20},{5,21},{6,22},{7,23},{8,24},{9,... | collective-permute-start | bytes 1572872 | tf_op jit(solution)/shard_map/ppermute | solution.py:155
  12.6 17.2 %collective-permute-start.3 = (bf16[4,128,512]{2,1,0:T(8,128)(2,1)S(1)}, bf16[4,128,512]{2,1,0:T(8,128)(2,1)S(1)}, u32[]{:S(2)}, u32[]{:S(2)}) collective-permute-start(bf16[4,128,512]{2,1,0:T(8,128)(2,1)S(1)} %pad_maximum_fusion.near_ref), channel_id=1, source_target_pairs={{0,4},{1,5},{2,6},{3,7},{4,8},{5,9},{6,10},{7,11},{8,12},{9,13},{1... | collective-permute-start | bytes 1572872 | tf_op jit(solution)/shard_map/ppermute | solution.py:138
  13.9 16.0 %collective-permute-start.4 = (bf16[4,128,512]{2,1,0:T(8,128)(2,1)S(1)}, bf16[4,128,512]{2,1,0:T(8,128)(2,1)S(1)}, u32[]{:S(2)}, u32[]{:S(2)}) collective-permute-start(bf16[4,128,512]{2,1,0:T(8,128)(2,1)S(1)} %pad_maximum_fusion.near_ref), channel_id=1, source_target_pairs={{0,8},{1,9},{2,10},{3,11},{4,12},{5,13},{6,14},{7,15},{8,0},{9,1},... | collective-permute-start | bytes 1572872 | tf_op jit(solution)/shard_map/ppermute | solution.py:138
  16.4 13.5 %collective-permute-start.5 = (bf16[4,128,512]{2,1,0:T(8,128)(2,1)S(1)}, bf16[4,128,512]{2,1,0:T(8,128)(2,1)S(1)}, u32[]{:S(2)}, u32[]{:S(2)}) collective-permute-start(bf16[4,128,512]{2,1,0:T(8,128)(2,1)S(1)} %pad_maximum_fusion.near_ref), channel_id=1, source_target_pairs={{0,12},{1,13},{2,14},{3,15},{4,0},{5,1},{6,2},{7,3},{8,4},{9,5},{1... | collective-permute-start | bytes 1572872 | tf_op jit(solution)/shard_map/ppermute | solution.py:138
  17.5 10.8 %collective-permute-start.7 = (f32[1,512]{1,0:T(1,128)S(1)}, f32[1,512]{1,0:T(1,128)S(1)}, u32[]{:S(2)}, u32[]{:S(2)}) collective-permute-start(f32[1,512]{1,0:T(1,128)S(1)} %copy-done.3), channel_id=1, source_target_pairs={{0,16},{1,17},{2,18},{3,19},{4,20},{5,21},{6,22},{7,23},{8,24},{9,... | collective-permute-start | bytes 6152 | tf_op jit(solution)/shard_map/ppermute | solution.py:156
  33.4 9.4 %collective-permute-start.11 = (bf16[128,512]{1,0:T(8,128)(2,1)S(1)}, bf16[128,512]{1,0:T(8,128)(2,1)S(1)}, u32[]{:S(2)}, u32[]{:S(2)}) collective-permute-start(bf16[128,512]{1,0:T(8,128)(2,1)S(1)} %get-tuple-element.24), channel_id=1, source_target_pairs={{0,124},{1,125},{2,126},{3,127},{4,112},{5,113},{6,114},{7,115},{8... | collective-permute-start | bytes 393224 | tf_op jit(solution)/shard_map/ppermute | solution.py:138
  35.2 7.5 %collective-permute-start.10 = (bf16[128,512]{1,0:T(8,128)(2,1)S(1)}, bf16[128,512]{1,0:T(8,128)(2,1)S(1)}, u32[]{:S(2)}, u32[]{:S(2)}) collective-permute-start(bf16[128,512]{1,0:T(8,128)(2,1)S(1)} %get-tuple-element.24), channel_id=1, source_target_pairs={{0,120},{1,121},{2,122},{3,123},{4,124},{5,125},{6,126},{7,127},{8... | collective-permute-start | bytes 393224 | tf_op jit(solution)/shard_map/ppermute | solution.py:138
  47.2 9.6 %collective-permute-start.12 = (bf16[4,128,512]{2,1,0:T(8,128)(2,1)S(1)}, bf16[4,128,512]{2,1,0:T(8,128)(2,1)S(1)}, u32[]{:S(2)}, u32[]{:S(2)}) collective-permute-start(bf16[4,128,512]{2,1,0:T(8,128)(2,1)S(1)} %pad_maximum_fusion.1.near_ref), channel_id=1, source_target_pairs={{0,4},{1,5},{2,6},{3,7},{4,8},{5,9},{6,10},{7,11},{8,12},{9,13},{1... | collective-permute-start | bytes 1572872 | tf_op jit(solution)/shard_map/ppermute | solution.py:138
  47.3 15.1 %collective-permute-start.13 = (bf16[4,128,512]{2,1,0:T(8,128)(2,1)S(1)}, bf16[4,128,512]{2,1,0:T(8,128)(2,1)S(1)}, u32[]{:S(2)}, u32[]{:S(2)}) collective-permute-start(bf16[4,128,512]{2,1,0:T(8,128)(2,1)S(1)} %pad_maximum_fusion.1.near_ref), channel_id=1, source_target_pairs={{0,8},{1,9},{2,10},{3,11},{4,12},{5,13},{6,14},{7,15},{8,0},{9,1},... | collective-permute-start | bytes 1572872 | tf_op jit(solution)/shard_map/ppermute | solution.py:138
  50.0 13.1 %collective-permute-start.14 = (bf16[4,128,512]{2,1,0:T(8,128)(2,1)S(1)}, bf16[4,128,512]{2,1,0:T(8,128)(2,1)S(1)}, u32[]{:S(2)}, u32[]{:S(2)}) collective-permute-start(bf16[4,128,512]{2,1,0:T(8,128)(2,1)S(1)} %pad_maximum_fusion.1.near_ref), channel_id=1, source_target_pairs={{0,12},{1,13},{2,14},{3,15},{4,0},{5,1},{6,2},{7,3},{8,4},{9,5},{1... | collective-permute-start | bytes 1572872 | tf_op jit(solution)/shard_map/ppermute | solution.py:138
  68.1 6.8 %collective-permute-start.17 = (bf16[128,512]{1,0:T(8,128)(2,1)S(1)}, bf16[128,512]{1,0:T(8,128)(2,1)S(1)}, u32[]{:S(2)}, u32[]{:S(2)}) collective-permute-start(bf16[128,512]{1,0:T(8,128)(2,1)S(1)} %get-tuple-element.26), channel_id=1, source_target_pairs={{0,120},{1,121},{2,122},{3,123},{4,124},{5,125},{6,126},{7,127},{8... | collective-permute-start | bytes 393224 | tf_op jit(solution)/shard_map/ppermute | solution.py:138
  78.2 9.6 %collective-permute-start.19 = (bf16[4,128,512]{2,1,0:T(8,128)(2,1)S(1)}, bf16[4,128,512]{2,1,0:T(8,128)(2,1)S(1)}, u32[]{:S(2)}, u32[]{:S(2)}) collective-permute-start(bf16[4,128,512]{2,1,0:T(8,128)(2,1)S(1)} %pad_maximum_fusion.2.near_ref), channel_id=1, source_target_pairs={{0,4},{1,5},{2,6},{3,7},{4,8},{5,9},{6,10},{7,11},{8,12},{9,13},{1... | collective-permute-start | bytes 1572872 | tf_op jit(solution)/shard_map/ppermute | solution.py:138
  80.2 13.5 %collective-permute-start.20 = (bf16[4,128,512]{2,1,0:T(8,128)(2,1)S(1)}, bf16[4,128,512]{2,1,0:T(8,128)(2,1)S(1)}, u32[]{:S(2)}, u32[]{:S(2)}) collective-permute-start(bf16[4,128,512]{2,1,0:T(8,128)(2,1)S(1)} %pad_maximum_fusion.2.near_ref), channel_id=1, source_target_pairs={{0,8},{1,9},{2,10},{3,11},{4,12},{5,13},{6,14},{7,15},{8,0},{9,1},... | collective-permute-start | bytes 1572872 | tf_op jit(solution)/shard_map/ppermute | solution.py:138
  81.2 12.8 %collective-permute-start.21 = (bf16[4,128,512]{2,1,0:T(8,128)(2,1)S(1)}, bf16[4,128,512]{2,1,0:T(8,128)(2,1)S(1)}, u32[]{:S(2)}, u32[]{:S(2)}) collective-permute-start(bf16[4,128,512]{2,1,0:T(8,128)(2,1)S(1)} %pad_maximum_fusion.2.near_ref), channel_id=1, source_target_pairs={{0,12},{1,13},{2,14},{3,15},{4,0},{5,1},{6,2},{7,3},{8,4},{9,5},{1... | collective-permute-start | bytes 1572872 | tf_op jit(solution)/shard_map/ppermute | solution.py:138
  100.2 6.9 %collective-permute-start.24 = (bf16[128,512]{1,0:T(8,128)(2,1)S(1)}, bf16[128,512]{1,0:T(8,128)(2,1)S(1)}, u32[]{:S(2)}, u32[]{:S(2)}) collective-permute-start(bf16[128,512]{1,0:T(8,128)(2,1)S(1)} %get-tuple-element.28), channel_id=1, source_target_pairs={{0,120},{1,121},{2,122},{3,123},{4,124},{5,125},{6,126},{7,127},{8... | collective-permute-start | bytes 393224 | tf_op jit(solution)/shard_map/ppermute | solution.py:138
  102.7 7.1 %collective-permute-start.22 = (bf16[128,512]{1,0:T(8,128)(2,1)S(1)}, bf16[128,512]{1,0:T(8,128)(2,1)S(1)}, u32[]{:S(2)}, u32[]{:S(2)}) collective-permute-start(bf16[128,512]{1,0:T(8,128)(2,1)S(1)} %get-tuple-element.28), channel_id=1, source_target_pairs={{0,112},{1,113},{2,114},{3,115},{4,116},{5,117},{6,118},{7,119},{8... | collective-permute-start | bytes 393224 | tf_op jit(solution)/shard_map/ppermute | solution.py:138
  109.9 14.9 %collective-permute-start.26 = (bf16[4,128,512]{2,1,0:T(8,128)(2,1)S(1)}, bf16[4,128,512]{2,1,0:T(8,128)(2,1)S(1)}, u32[]{:S(2)}, u32[]{:S(2)}) collective-permute-start(bf16[4,128,512]{2,1,0:T(8,128)(2,1)S(1)} %pad_maximum_fusion.3.near_ref), channel_id=1, source_target_pairs={{0,4},{1,5},{2,6},{3,7},{4,8},{5,9},{6,10},{7,11},{8,12},{9,13},{1... | collective-permute-start | bytes 1572872 | tf_op jit(solution)/shard_map/ppermute | solution.py:138
  111.3 13.5 %collective-permute-start.27 = (bf16[4,128,512]{2,1,0:T(8,128)(2,1)S(1)}, bf16[4,128,512]{2,1,0:T(8,128)(2,1)S(1)}, u32[]{:S(2)}, u32[]{:S(2)}) collective-permute-start(bf16[4,128,512]{2,1,0:T(8,128)(2,1)S(1)} %pad_maximum_fusion.3.near_ref), channel_id=1, source_target_pairs={{0,8},{1,9},{2,10},{3,11},{4,12},{5,13},{6,14},{7,15},{8,0},{9,1},... | collective-permute-start | bytes 1572872 | tf_op jit(solution)/shard_map/ppermute | solution.py:138
  112.3 13.3 %collective-permute-start.28 = (bf16[4,128,512]{2,1,0:T(8,128)(2,1)S(1)}, bf16[4,128,512]{2,1,0:T(8,128)(2,1)S(1)}, u32[]{:S(2)}, u32[]{:S(2)}) collective-permute-start(bf16[4,128,512]{2,1,0:T(8,128)(2,1)S(1)} %pad_maximum_fusion.3.near_ref), channel_id=1, source_target_pairs={{0,12},{1,13},{2,14},{3,15},{4,0},{5,1},{6,2},{7,3},{8,4},{9,5},{1... | collective-permute-start | bytes 1572872 | tf_op jit(solution)/shard_map/ppermute | solution.py:138
  130.6 6.9 %collective-permute-start.31 = (bf16[128,512]{1,0:T(8,128)(2,1)S(1)}, bf16[128,512]{1,0:T(8,128)(2,1)S(1)}, u32[]{:S(2)}, u32[]{:S(2)}) collective-permute-start(bf16[128,512]{1,0:T(8,128)(2,1)S(1)} %get-tuple-element.30), channel_id=1, source_target_pairs={{0,120},{1,121},{2,122},{3,123},{4,124},{5,125},{6,126},{7,127},{8... | collective-permute-start | bytes 393224 | tf_op jit(solution)/shard_map/ppermute | solution.py:138
  140.3 9.5 %collective-permute-start.33 = (bf16[4,128,512]{2,1,0:T(8,128)(2,1)S(1)}, bf16[4,128,512]{2,1,0:T(8,128)(2,1)S(1)}, u32[]{:S(2)}, u32[]{:S(2)}) collective-permute-start(bf16[4,128,512]{2,1,0:T(8,128)(2,1)S(1)} %pad_maximum_fusion.4.near_ref), channel_id=1, source_target_pairs={{0,4},{1,5},{2,6},{3,7},{4,8},{5,9},{6,10},{7,11},{8,12},{9,13},{1... | collective-permute-start | bytes 1572872 | tf_op jit(solution)/shard_map/ppermute | solution.py:138
  141.9 13.9 %collective-permute-start.34 = (bf16[4,128,512]{2,1,0:T(8,128)(2,1)S(1)}, bf16[4,128,512]{2,1,0:T(8,128)(2,1)S(1)}, u32[]{:S(2)}, u32[]{:S(2)}) collective-permute-start(bf16[4,128,512]{2,1,0:T(8,128)(2,1)S(1)} %pad_maximum_fusion.4.near_ref), channel_id=1, source_target_pairs={{0,8},{1,9},{2,10},{3,11},{4,12},{5,13},{6,14},{7,15},{8,0},{9,1},... | collective-permute-start | bytes 1572872 | tf_op jit(solution)/shard_map/ppermute | solution.py:138
  143.3 12.8 %collective-permute-start.35 = (bf16[4,128,512]{2,1,0:T(8,128)(2,1)S(1)}, bf16[4,128,512]{2,1,0:T(8,128)(2,1)S(1)}, u32[]{:S(2)}, u32[]{:S(2)}) collective-permute-start(bf16[4,128,512]{2,1,0:T(8,128)(2,1)S(1)} %pad_maximum_fusion.4.near_ref), channel_id=1, source_target_pairs={{0,12},{1,13},{2,14},{3,15},{4,0},{5,1},{6,2},{7,3},{8,4},{9,5},{1... | collective-permute-start | bytes 1572872 | tf_op jit(solution)/shard_map/ppermute | solution.py:138
  161.2 6.9 %collective-permute-start.38 = (bf16[128,512]{1,0:T(8,128)(2,1)S(1)}, bf16[128,512]{1,0:T(8,128)(2,1)S(1)}, u32[]{:S(2)}, u32[]{:S(2)}) collective-permute-start(bf16[128,512]{1,0:T(8,128)(2,1)S(1)} %get-tuple-element.32), channel_id=1, source_target_pairs={{0,120},{1,121},{2,122},{3,123},{4,124},{5,125},{6,126},{7,127},{8... | collective-permute-start | bytes 393224 | tf_op jit(solution)/shard_map/ppermute | solution.py:138
  171.0 9.6 %collective-permute-start.40 = (bf16[4,128,512]{2,1,0:T(8,128)(2,1)S(1)}, bf16[4,128,512]{2,1,0:T(8,128)(2,1)S(1)}, u32[]{:S(2)}, u32[]{:S(2)}) collective-permute-start(bf16[4,128,512]{2,1,0:T(8,128)(2,1)S(1)} %pad_maximum_fusion.5.near_ref), channel_id=1, source_target_pairs={{0,4},{1,5},{2,6},{3,7},{4,8},{5,9},{6,10},{7,11},{8,12},{9,13},{1... | collective-permute-start | bytes 1572872 | tf_op jit(solution)/shard_map/ppermute | solution.py:138
  173.0 13.5 %collective-permute-start.41 = (bf16[4,128,512]{2,1,0:T(8,128)(2,1)S(1)}, bf16[4,128,512]{2,1,0:T(8,128)(2,1)S(1)}, u32[]{:S(2)}, u32[]{:S(2)}) collective-permute-start(bf16[4,128,512]{2,1,0:T(8,128)(2,1)S(1)} %pad_maximum_fusion.5.near_ref), channel_id=1, source_target_pairs={{0,8},{1,9},{2,10},{3,11},{4,12},{5,13},{6,14},{7,15},{8,0},{9,1},... | collective-permute-start | bytes 1572872 | tf_op jit(solution)/shard_map/ppermute | solution.py:138
  174.0 12.8 %collective-permute-start.42 = (bf16[4,128,512]{2,1,0:T(8,128)(2,1)S(1)}, bf16[4,128,512]{2,1,0:T(8,128)(2,1)S(1)}, u32[]{:S(2)}, u32[]{:S(2)}) collective-permute-start(bf16[4,128,512]{2,1,0:T(8,128)(2,1)S(1)} %pad_maximum_fusion.5.near_ref), channel_id=1, source_target_pairs={{0,12},{1,13},{2,14},{3,15},{4,0},{5,1},{6,2},{7,3},{8,4},{9,5},{1... | collective-permute-start | bytes 1572872 | tf_op jit(solution)/shard_map/ppermute | solution.py:138
  192.2 6.9 %collective-permute-start.45 = (bf16[128,512]{1,0:T(8,128)(2,1)S(1)}, bf16[128,512]{1,0:T(8,128)(2,1)S(1)}, u32[]{:S(2)}, u32[]{:S(2)}) collective-permute-start(bf16[128,512]{1,0:T(8,128)(2,1)S(1)} %get-tuple-element.34), channel_id=1, source_target_pairs={{0,120},{1,121},{2,122},{3,123},{4,124},{5,125},{6,126},{7,127},{8... | collective-permute-start | bytes 393224 | tf_op jit(solution)/shard_map/ppermute | solution.py:138
  201.9 9.6 %collective-permute-start.47 = (bf16[4,128,512]{2,1,0:T(8,128)(2,1)S(1)}, bf16[4,128,512]{2,1,0:T(8,128)(2,1)S(1)}, u32[]{:S(2)}, u32[]{:S(2)}) collective-permute-start(bf16[4,128,512]{2,1,0:T(8,128)(2,1)S(1)} %pad_maximum_fusion.6.near_ref), channel_id=1, source_target_pairs={{0,4},{1,5},{2,6},{3,7},{4,8},{5,9},{6,10},{7,11},{8,12},{9,13},{1... | collective-permute-start | bytes 1572872 | tf_op jit(solution)/shard_map/ppermute | solution.py:138
  203.9 13.2 %collective-permute-start.48 = (bf16[4,128,512]{2,1,0:T(8,128)(2,1)S(1)}, bf16[4,128,512]{2,1,0:T(8,128)(2,1)S(1)}, u32[]{:S(2)}, u32[]{:S(2)}) collective-permute-start(bf16[4,128,512]{2,1,0:T(8,128)(2,1)S(1)} %pad_maximum_fusion.6.near_ref), channel_id=1, source_target_pairs={{0,8},{1,9},{2,10},{3,11},{4,12},{5,13},{6,14},{7,15},{8,0},{9,1},... | collective-permute-start | bytes 1572872 | tf_op jit(solution)/shard_map/ppermute | solution.py:138
  204.7 13.1 %collective-permute-start.49 = (bf16[4,128,512]{2,1,0:T(8,128)(2,1)S(1)}, bf16[4,128,512]{2,1,0:T(8,128)(2,1)S(1)}, u32[]{:S(2)}, u32[]{:S(2)}) collective-permute-start(bf16[4,128,512]{2,1,0:T(8,128)(2,1)S(1)} %pad_maximum_fusion.6.near_ref), channel_id=1, source_target_pairs={{0,12},{1,13},{2,14},{3,15},{4,0},{5,1},{6,2},{7,3},{8,4},{9,5},{1... | collective-permute-start | bytes 1572872 | tf_op jit(solution)/shard_map/ppermute | solution.py:138
  223.2 6.9 %collective-permute-start.52 = (bf16[128,512]{1,0:T(8,128)(2,1)S(1)}, bf16[128,512]{1,0:T(8,128)(2,1)S(1)}, u32[]{:S(2)}, u32[]{:S(2)}) collective-permute-start(bf16[128,512]{1,0:T(8,128)(2,1)S(1)} %get-tuple-element.36), channel_id=1, source_target_pairs={{0,120},{1,121},{2,122},{3,123},{4,124},{5,125},{6,126},{7,127},{8... | collective-permute-start | bytes 393224 | tf_op jit(solution)/shard_map/ppermute | solution.py:138
  232.9 9.6 %collective-permute-start.54 = (bf16[4,128,512]{2,1,0:T(8,128)(2,1)S(1)}, bf16[4,128,512]{2,1,0:T(8,128)(2,1)S(1)}, u32[]{:S(2)}, u32[]{:S(2)}) collective-permute-start(bf16[4,128,512]{2,1,0:T(8,128)(2,1)S(1)} %pad_maximum_fusion.7.near_ref), channel_id=1, source_target_pairs={{0,4},{1,5},{2,6},{3,7},{4,8},{5,9},{6,10},{7,11},{8,12},{9,13},{1... | collective-permute-start | bytes 1572872 | tf_op jit(solution)/shard_map/ppermute | solution.py:138
  234.9 13.4 %collective-permute-start.55 = (bf16[4,128,512]{2,1,0:T(8,128)(2,1)S(1)}, bf16[4,128,512]{2,1,0:T(8,128)(2,1)S(1)}, u32[]{:S(2)}, u32[]{:S(2)}) collective-permute-start(bf16[4,128,512]{2,1,0:T(8,128)(2,1)S(1)} %pad_maximum_fusion.7.near_ref), channel_id=1, source_target_pairs={{0,8},{1,9},{2,10},{3,11},{4,12},{5,13},{6,14},{7,15},{8,0},{9,1},... | collective-permute-start | bytes 1572872 | tf_op jit(solution)/shard_map/ppermute | solution.py:138
  235.8 13.0 %collective-permute-start.56 = (bf16[4,128,512]{2,1,0:T(8,128)(2,1)S(1)}, bf16[4,128,512]{2,1,0:T(8,128)(2,1)S(1)}, u32[]{:S(2)}, u32[]{:S(2)}) collective-permute-start(bf16[4,128,512]{2,1,0:T(8,128)(2,1)S(1)} %pad_maximum_fusion.7.near_ref), channel_id=1, source_target_pairs={{0,12},{1,13},{2,14},{3,15},{4,0},{5,1},{6,2},{7,3},{8,4},{9,5},{1... | collective-permute-start | bytes 1572872 | tf_op jit(solution)/shard_map/ppermute | solution.py:138
  254.3 7.0 %collective-permute-start.59 = (bf16[128,512]{1,0:T(8,128)(2,1)S(1)}, bf16[128,512]{1,0:T(8,128)(2,1)}, u32[]{:S(2)}, u32[]{:S(2)}) collective-permute-start(bf16[128,512]{1,0:T(8,128)(2,1)S(1)} %get-tuple-element.38), channel_id=1, source_target_pairs={{0,120},{1,121},{2,122},{3,123},{4,124},{5,125},{6,126},{7,127},{8... | collective-permute-start | bytes 393224 | tf_op jit(solution)/shard_map/ppermute | solution.py:138
  265.1 11.3 %collective-permute-start.61 = (bf16[4,128,512]{2,1,0:T(8,128)(2,1)S(1)}, bf16[4,128,512]{2,1,0:T(8,128)(2,1)S(1)}, u32[]{:S(2)}, u32[]{:S(2)}) collective-permute-start(bf16[4,128,512]{2,1,0:T(8,128)(2,1)S(1)} %pad_maximum_fusion.8.near_ref), channel_id=1, source_target_pairs={{0,4},{1,5},{2,6},{3,7},{4,8},{5,9},{6,10},{7,11},{8,12},{9,13},{1... | collective-permute-start | bytes 1572872 | tf_op jit(solution)/shard_map/ppermute | solution.py:138
  266.9 13.4 %collective-permute-start.62 = (bf16[4,128,512]{2,1,0:T(8,128)(2,1)S(1)}, bf16[4,128,512]{2,1,0:T(8,128)(2,1)S(1)}, u32[]{:S(2)}, u32[]{:S(2)}) collective-permute-start(bf16[4,128,512]{2,1,0:T(8,128)(2,1)S(1)} %pad_maximum_fusion.8.near_ref), channel_id=1, source_target_pairs={{0,8},{1,9},{2,10},{3,11},{4,12},{5,13},{6,14},{7,15},{8,0},{9,1},... | collective-permute-start | bytes 1572872 | tf_op jit(solution)/shard_map/ppermute | solution.py:138
  268.0 13.0 %collective-permute-start.63 = (bf16[4,128,512]{2,1,0:T(8,128)(2,1)S(1)}, bf16[4,128,512]{2,1,0:T(8,128)(2,1)S(1)}, u32[]{:S(2)}, u32[]{:S(2)}) collective-permute-start(bf16[4,128,512]{2,1,0:T(8,128)(2,1)S(1)} %pad_maximum_fusion.8.near_ref), channel_id=1, source_target_pairs={{0,12},{1,13},{2,14},{3,15},{4,0},{5,1},{6,2},{7,3},{8,4},{9,5},{1... | collective-permute-start | bytes 1572872 | tf_op jit(solution)/shard_map/ppermute | solution.py:138
  286.2 6.8 %collective-permute-start.66 = (bf16[128,512]{1,0:T(8,128)(2,1)S(1)}, bf16[128,512]{1,0:T(8,128)(2,1)S(1)}, u32[]{:S(2)}, u32[]{:S(2)}) collective-permute-start(bf16[128,512]{1,0:T(8,128)(2,1)S(1)} %get-tuple-element.40), channel_id=1, source_target_pairs={{0,120},{1,121},{2,122},{3,123},{4,124},{5,125},{6,126},{7,127},{8... | collective-permute-start | bytes 393224 | tf_op jit(solution)/shard_map/ppermute | solution.py:138
  296.1 9.5 %collective-permute-start.68 = (bf16[4,128,512]{2,1,0:T(8,128)(2,1)S(1)}, bf16[4,128,512]{2,1,0:T(8,128)(2,1)S(1)}, u32[]{:S(2)}, u32[]{:S(2)}) collective-permute-start(bf16[4,128,512]{2,1,0:T(8,128)(2,1)S(1)} %pad_maximum_fusion.9.near_ref), channel_id=1, source_target_pairs={{0,4},{1,5},{2,6},{3,7},{4,8},{5,9},{6,10},{7,11},{8,12},{9,13},{1... | collective-permute-start | bytes 1572872 | tf_op jit(solution)/shard_map/ppermute | solution.py:138
  297.6 13.7 %collective-permute-start.69 = (bf16[4,128,512]{2,1,0:T(8,128)(2,1)S(1)}, bf16[4,128,512]{2,1,0:T(8,128)(2,1)S(1)}, u32[]{:S(2)}, u32[]{:S(2)}) collective-permute-start(bf16[4,128,512]{2,1,0:T(8,128)(2,1)S(1)} %pad_maximum_fusion.9.near_ref), channel_id=1, source_target_pairs={{0,8},{1,9},{2,10},{3,11},{4,12},{5,13},{6,14},{7,15},{8,0},{9,1},... | collective-permute-start | bytes 1572872 | tf_op jit(solution)/shard_map/ppermute | solution.py:138
  299.1 12.8 %collective-permute-start.70 = (bf16[4,128,512]{2,1,0:T(8,128)(2,1)S(1)}, bf16[4,128,512]{2,1,0:T(8,128)(2,1)S(1)}, u32[]{:S(2)}, u32[]{:S(2)}) collective-permute-start(bf16[4,128,512]{2,1,0:T(8,128)(2,1)S(1)} %pad_maximum_fusion.9.near_ref), channel_id=1, source_target_pairs={{0,12},{1,13},{2,14},{3,15},{4,0},{5,1},{6,2},{7,3},{8,4},{9,5},{1... | collective-permute-start | bytes 1572872 | tf_op jit(solution)/shard_map/ppermute | solution.py:138
  316.9 6.8 %collective-permute-start.73 = (bf16[128,512]{1,0:T(8,128)(2,1)S(1)}, bf16[128,512]{1,0:T(8,128)(2,1)S(1)}, u32[]{:S(2)}, u32[]{:S(2)}) collective-permute-start(bf16[128,512]{1,0:T(8,128)(2,1)S(1)} %get-tuple-element.42), channel_id=1, source_target_pairs={{0,120},{1,121},{2,122},{3,123},{4,124},{5,125},{6,126},{7,127},{8... | collective-permute-start | bytes 393224 | tf_op jit(solution)/shard_map/ppermute | solution.py:138
  326.8 9.6 %collective-permute-start.75 = (bf16[4,128,512]{2,1,0:T(8,128)(2,1)S(1)}, bf16[4,128,512]{2,1,0:T(8,128)(2,1)S(1)}, u32[]{:S(2)}, u32[]{:S(2)}) collective-permute-start(bf16[4,128,512]{2,1,0:T(8,128)(2,1)S(1)} %pad_maximum_fusion.10.near_ref), channel_id=1, source_target_pairs={{0,4},{1,5},{2,6},{3,7},{4,8},{5,9},{6,10},{7,11},{8,12},{9,13},{1... | collective-permute-start | bytes 1572872 | tf_op jit(solution)/shard_map/ppermute | solution.py:138
  328.6 13.6 %collective-permute-start.76 = (bf16[4,128,512]{2,1,0:T(8,128)(2,1)S(1)}, bf16[4,128,512]{2,1,0:T(8,128)(2,1)S(1)}, u32[]{:S(2)}, u32[]{:S(2)}) collective-permute-start(bf16[4,128,512]{2,1,0:T(8,128)(2,1)S(1)} %pad_maximum_fusion.10.near_ref), channel_id=1, source_target_pairs={{0,8},{1,9},{2,10},{3,11},{4,12},{5,13},{6,14},{7,15},{8,0},{9,1},... | collective-permute-start | bytes 1572872 | tf_op jit(solution)/shard_map/ppermute | solution.py:138
  329.8 12.8 %collective-permute-start.77 = (bf16[4,128,512]{2,1,0:T(8,128)(2,1)S(1)}, bf16[4,128,512]{2,1,0:T(8,128)(2,1)S(1)}, u32[]{:S(2)}, u32[]{:S(2)}) collective-permute-start(bf16[4,128,512]{2,1,0:T(8,128)(2,1)S(1)} %pad_maximum_fusion.10.near_ref), channel_id=1, source_target_pairs={{0,12},{1,13},{2,14},{3,15},{4,0},{5,1},{6,2},{7,3},{8,4},{9,5},{1... | collective-permute-start | bytes 1572872 | tf_op jit(solution)/shard_map/ppermute | solution.py:138
  (34 other events, 433.6 us)

commit v2 on v1

v2 whole, which is shorter than its diff:
```python
import math

import jax
import jax.numpy as jnp
from jax import lax
from jax.experimental import pallas as pl
from jax.experimental.pallas import tpu as pltpu
from jax.sharding import PartitionSpec as P

AXES = ("layer", "front")
BLOCKS = 4
HOP_FIRST = False
NEAR_ORDER = (1, 3, 2, 0)
FAR_ORDER = (2, 3, 1)
USE_ORDER = (1, 3, 2)
SIDE = 4
IN_VMEM = pl.BlockSpec(memory_space=pltpu.VMEM)
IN_SMEM = pl.BlockSpec(memory_space=pltpu.SMEM)
IN_HBM = pl.BlockSpec(memory_space=pltpu.HBM)


def arrange(factor, order):
    rows, columns = factor.shape
    fronts = order.shape[0]
    width = columns // fronts

    def body(order_ref, source, *refs):
        targets, sem = refs[:SIDE], refs[SIDE]

        def copy(i):
            start = pl.multiple_of(order_ref[i] * width, width)
            return pltpu.make_async_copy(
                source.at[:, pl.ds(start, width)],
                targets[i // SIDE].at[:, pl.ds(i % SIDE * width, width)],
                sem.at[i],
            )

        for i in range(fronts):
            copy(i).start()
        for i in range(fronts):
            copy(i).wait()

    return pl.pallas_call(
        body,
        in_specs=[IN_SMEM, IN_HBM],
        out_specs=(IN_VMEM,) * SIDE,
        out_shape=(pltpu.VMEM((rows, columns // SIDE), factor.dtype),) * SIDE,
        scratch_shapes=[pltpu.SemaphoreType.DMA((fronts,))],
        compiler_params=pltpu.CompilerParams(vmem_limit_bytes=32 << 20),
        cost_estimate=pl.CostEstimate(flops=0, bytes_accessed=2 * rows * columns, transcendentals=0),
        name="arrange",
    )(order, factor)


def kept(value):
    return pltpu.with_memory_space_constraint(value, pltpu.VMEM)


def term(panel_ref, pieces_ref):
    joined = jnp.concatenate([pieces_ref[i] for i in range(SIDE)], axis=1)
    return lax.dot_general(
        panel_ref[...], joined, (((1,), (1,)), ((), ())), preferred_element_type=jnp.float32
    )


def add_product(panel, total, pieces):
    rows, columns = panel.shape
    height = pieces.shape[1]
    totals = () if total is None else (kept(total),)

    def body(panel_ref, pieces_ref, *refs):
        product = term(panel_ref, pieces_ref)
        refs[-1][...] = product if total is None else refs[0][...] + product

    return pl.pallas_call(
        body,
        in_specs=[IN_VMEM] * (2 + len(totals)),
        out_specs=IN_VMEM,
        out_shape=pltpu.VMEM((rows, height), jnp.float32),
        compiler_params=pltpu.CompilerParams(vmem_limit_bytes=16 << 20),
        cost_estimate=pl.CostEstimate(
            flops=2 * rows * columns * height, bytes_accessed=2 * rows * columns, transcendentals=0
        ),
        name="add_product",
    )(kept(panel), pieces, *totals)


def finish_product(panel, total, pieces, rhs, couple):
    rows, columns = panel.shape
    height = total.shape[1]
    half, middle = height // 2, rows // 2

    def body(panel_ref, total_ref, pieces_ref, rhs_ref, couple_ref, field_ref, merged_ref):
        total = total_ref[...] + term(panel_ref, pieces_ref)
        plain = total[:middle].T
        twisted = total[middle:].T
        field = jnp.concatenate(
            (plain[:half] - twisted[half:], plain[half:] + twisted[:half]), axis=0
        ).astype(field_ref.dtype)
        field_ref[...] = field
        merged = rhs_ref[...].astype(jnp.float32) + couple_ref[...] * field.astype(jnp.float32)
        merged_ref[...] = merged.astype(merged_ref.dtype)

    shape = jax.ShapeDtypeStruct((height, middle), jnp.bfloat16)
    return pl.pallas_call(
        body,
        in_specs=[IN_VMEM] * 5,
        out_specs=(IN_VMEM, IN_VMEM),
        out_shape=(shape, shape),
        compiler_params=pltpu.CompilerParams(vmem_limit_bytes=16 << 20),
        cost_estimate=pl.CostEstimate(
            flops=2 * rows * columns * height, bytes_accessed=2 * rows * columns, transcendentals=0
        ),
        name="finish_product",
    )(kept(panel), kept(total), pieces, rhs, couple)


def on_device(factor, right_side, coupling, forward):
    layers, fronts = lax.axis_size("layer"), lax.axis_size("front")
    position = lax.axis_index("layer")
    place = lax.axis_index("front")
    rows, sources = right_side.shape[2:]
    count = BLOCKS
    block = sources // count
    steps = count + layers - 1

    def device(layer, slow, fast):
        return layer * fronts + slow * SIDE + fast

    def moves(down, near, far):
        pairs = []
        for layer in range(layers):
            reached = (layer - down) % layers
            slow_step, fast_step = (far, near) if reached % 2 == 0 else (near, far)
            for slow in range(SIDE):
                for fast in range(SIDE):
                    pairs.append(
                        (device(layer, slow, fast), device(reached, slow ^ slow_step, fast ^ fast_step))
                    )
        return pairs

    def moved(value, down, near, far):
        return lax.ppermute(value, AXES, moves(down, near, far))

    slow, fast = place // SIDE, place % SIDE
    even = position % 2 == 0
    order = []
    for far in range(SIDE):
        for near in range(SIDE):
            slow_step = jnp.where(even, far, near)
            fast_step = jnp.where(even, near, far)
            order.append((slow ^ slow_step) * SIDE + (fast ^ fast_step))
    order = jnp.stack(order).astype(jnp.int32)
    panels = arrange(factor[0].reshape(2 * rows, -1), order)

    turned = jnp.swapaxes(right_side[0], 1, 2)
    blocks = turned.reshape(2, count, block, rows).swapaxes(0, 1).reshape(count, 2 * block, rows)

    up = [(l * fronts + f, (l + 1) % layers * fronts + f) for l in range(layers) for f in range(fronts)]
    next_rhs = lax.ppermute(blocks, AXES, up)
    next_couple = jnp.where(position == 0, 0.0, lax.ppermute(coupling, AXES, up))
    depth = jnp.where(position == 0, layers, position)
    next_rhs = jnp.pad(next_rhs, ((layers - 2, layers - 1), (0, 0), (0, 0)))
    next_rhs = lax.dynamic_slice_in_dim(next_rhs, depth - 1, steps - 1, 0)

    fields = []
    merged = blocks[0]
    for step in range(steps):
        down = min(step, 1)
        if HOP_FIRST:
            own = moved(merged, 1, 0, 0) if down else merged
            near = {0: own} | {i: moved(own, 0, i, 0) for i in NEAR_ORDER if i}
        else:
            near = {i: merged if down == 0 and i == 0 else moved(merged, down, i, 0) for i in NEAR_ORDER}
        near = jnp.stack([near[i] for i in range(SIDE)])
        far = {i: moved(near, 0, 0, i) for i in FAR_ORDER}
        total = add_product(panels[0], None, near)
        for i in USE_ORDER[:-1]:
            total = add_product(panels[i], total, far[i])
        last = USE_ORDER[-1]
        rhs = next_rhs[min(step, steps - 2)]
        field, merged = finish_product(panels[last], total, far[last], rhs, next_couple)
        fields.append(field)

    result = lax.dynamic_slice_in_dim(jnp.stack(fields), layers - 1 - position, count, 0)
    result = result.reshape(count, 2, block, rows).swapaxes(0, 1).reshape(2, sources, rows)
    result = jnp.swapaxes(result, 1, 2)
    forward, result = lax.optimization_barrier((forward, result))
    field_fwd = forward[0].astype(jnp.float32)
    field_adj = result.astype(jnp.float32)
    gradient = jnp.sum(
        field_fwd[0] * field_adj[0] - field_fwd[1] * field_adj[1], axis=-1
    ) / math.sqrt(sources)
    return (result[None], gradient[None])


def solution(mesh):
    placed = (
        P("layer", None, "front", None),
        P("layer", None, "front", None),
        P("layer", "front"),
        P("layer", None, "front", None),
    )
    return jax.shard_map(
        on_device,
        mesh=mesh,
        in_specs=placed,
        out_specs=(P("layer", None, "front", None), P("layer", "front")),
        check_vma=False,
    )
```

time: 356 us -> 337 us (0.947)
  starting transfers between devices: 113 us -> 97.9 us
  Pallas kernels: 55 us -> 61.5 us
  waiting for transfers between devices: 164 us -> 160 us
    ppermute x76, starting transfers between devices: 106 us -> 90.9 us  [moved(): return lax.ppermute(value, AXES, moves(down, near, far))]
    pallas_call x22 -> x44, Pallas kernels: 55 us -> 61.5 us  [the longest x33 41.4 us: add_product(): pl.pallas_call(body, in_specs=[IN_VMEM] * (2 + len(totals)), out_specs=IN...]
    ppermute x76, waiting for transfers between devices: 164 us -> 160 us  [moved(): return lax.ppermute(value, AXES, moves(down, near, far))]
    unnamed x21 -> x32, local copies, waits for them, and re-layouts: 8.35 us -> 5.53 us
  transfers between devices with their start and end apart: 78 -> 78, of which waited for: 60 -> 53; matrix products, arithmetic and copies ran while one was open for 0% -> 0% of each run, Pallas kernels for 6% -> 15%
where the time goes in v2:
time: 337 us; the launch traced here: 331 us
  waiting for transfers between devices  160 us (47%)
  starting transfers between devices  97.9 us (29%)
  Pallas kernels  61.5 us (18%)
  local copies, waits for them, and re-layouts  6.22 us (2%)
  other arithmetic  3.82 us (1%)
    ppermute x76, waiting for transfers between devices, moved(): return lax.ppermute(value, AXES, moves(down, near, far))  160 us
    ppermute x76, starting transfers between devices, moved(): return lax.ppermute(value, AXES, moves(down, near, far))  90.9 us
    pallas_call x33, Pallas kernels, add_product(): pl.pallas_call(body, in_specs=[IN_VMEM] * (2 + len(totals)), out_specs=IN...  41.4 us
    pallas_call x10, Pallas kernels, finish_product(): pl.pallas_call(body, in_specs=[IN_VMEM] * 5, out_specs=(IN_VMEM, IN_VMEM)...  13.5 us
  transfers between devices with their start and end apart: 78, of which 53 were waited for; matrix products, arithmetic and copies ran while one was open for 0% of the time, Pallas kernels for 15%

profile of v2, /device:TPU:1, one launch (start us, length us, event | category | flops | bytes accessed | tf_op | source)
XLA Modules:
  0.0 330.7 jit_solution(8605770607467757428)
XLA Ops:
  1.9 2.2 collective-permute-start
  4.1 2.6 collective-permute-start.1
  6.8 3.0 collective-permute-start.6
  15.4 4.0 %collective-permute-start.7 = (f32[1,512]{1,0:T(1,128)S(1)}, f32[1,512]{1,0:T(1,128)S(1)}, u32[]{:S(2)}, u32[]{:S(2)}) collective-permute-start(f32[1,512]{1,0:T(1,128)S(1)} %copy-done.9), channel_id=1, source_target_pairs={{0,16},{1,17},{2,18},{3,19},{4,20},{5,21},{6,22},{7,23},{8,24},{9,... | collective-permute-start | bytes 6152 | tf_op jit(solution)/shard_map/ppermute | solution.py:161
  20.1 6.6 %arrange.1 = (bf16[1024,2048]{1,0:T(8,128)(2,1)S(1)}, bf16[1024,2048]{1,0:T(8,128)(2,1)S(1)}, bf16[1024,2048]{1,0:T(8,128)(2,1)S(1)}, bf16[1024,2048]{1,0:T(8,128)(2,1)S(1)}) custom-call(s32[16]{0:T(128)S(1)} %stack.265.order_ref, bf16[1024,8192]{1,0:T(8,128)(2,1)} %bitcast.129), custom_call_target="tpu_custom_call" | custom-call | bytes 16777216 | tf_op jit(solution)/shard_map/arrange/pallas_call | solution.py:43
  32.3 2.0 collective-permute-start.8
  34.3 3.3 %collective-permute-start.10 = (bf16[128,512]{1,0:T(8,128)(2,1)S(1)}, bf16[128,512]{1,0:T(8,128)(2,1)S(1)}, u32[]{:S(2)}, u32[]{:S(2)}) collective-permute-start(bf16[128,512]{1,0:T(8,128)(2,1)S(1)} %get-tuple-element.34), channel_id=1, source_target_pairs={{0,120},{1,121},{2,122},{3,123},{4,124},{5,125},{6,126},{7,127},{8... | collective-permute-start | bytes 393224 | tf_op jit(solution)/shard_map/ppermute | solution.py:143
  37.6 2.8 collective-permute-start.11
  40.4 2.2 collective-permute-done.10
  49.0 3.7 %collective-permute-done.13.pieces_ref = bf16[4,128,512]{2,1,0:T(8,128)(2,1)S(1)} collective-permute-done((bf16[4,128,512]{2,1,0:T(8,128)(2,1)S(1)}, bf16[4,128,512]{2,1,0:T(8,128)(2,1)S(1)}, u32[]{:S(2)}, u32[]{:S(2)}) %collective-permute-start.13) | collective-permute-done | bytes 524320 | tf_op jit(solution)/shard_map/ppermute | solution.py:143
  53.9 6.2 %collective-permute-done.12.pieces_ref = bf16[4,128,512]{2,1,0:T(8,128)(2,1)S(1)} collective-permute-done((bf16[4,128,512]{2,1,0:T(8,128)(2,1)S(1)}, bf16[4,128,512]{2,1,0:T(8,128)(2,1)S(1)}, u32[]{:S(2)}, u32[]{:S(2)}) %collective-permute-start.12) | collective-permute-done | bytes 524320 | tf_op jit(solution)/shard_map/ppermute | solution.py:143
  62.7 3.3 collective-permute-start.15
  68.9 2.4 collective-permute-done.16
  71.3 2.8 collective-permute-done.17
  79.6 3.8 %collective-permute-done.20.pieces_ref = bf16[4,128,512]{2,1,0:T(8,128)(2,1)S(1)} collective-permute-done((bf16[4,128,512]{2,1,0:T(8,128)(2,1)S(1)}, bf16[4,128,512]{2,1,0:T(8,128)(2,1)S(1)}, u32[]{:S(2)}, u32[]{:S(2)}) %collective-permute-start.20) | collective-permute-done | bytes 524320 | tf_op jit(solution)/shard_map/ppermute | solution.py:143
  84.7 6.6 %collective-permute-done.19.pieces_ref = bf16[4,128,512]{2,1,0:T(8,128)(2,1)S(1)} collective-permute-done((bf16[4,128,512]{2,1,0:T(8,128)(2,1)S(1)}, bf16[4,128,512]{2,1,0:T(8,128)(2,1)S(1)}, u32[]{:S(2)}, u32[]{:S(2)}) %collective-permute-start.19) | collective-permute-done | bytes 524320 | tf_op jit(solution)/shard_map/ppermute | solution.py:143
  95.8 4.2 %collective-permute-done.22 = bf16[128,512]{1,0:T(8,128)(2,1)S(1)} collective-permute-done((bf16[128,512]{1,0:T(8,128)(2,1)S(1)}, bf16[128,512]{1,0:T(8,128)(2,1)S(1)}, u32[]{:S(2)}, u32[]{:S(2)}) %collective-permute-start.22) | collective-permute-done | bytes 131104 | tf_op jit(solution)/shard_map/ppermute | solution.py:143
  100.0 2.5 collective-permute-done.24
  108.3 3.8 %collective-permute-done.27.pieces_ref = bf16[4,128,512]{2,1,0:T(8,128)(2,1)S(1)} collective-permute-done((bf16[4,128,512]{2,1,0:T(8,128)(2,1)S(1)}, bf16[4,128,512]{2,1,0:T(8,128)(2,1)S(1)}, u32[]{:S(2)}, u32[]{:S(2)}) %collective-permute-start.27) | collective-permute-done | bytes 524320 | tf_op jit(solution)/shard_map/ppermute | solution.py:143
  113.4 6.3 %collective-permute-done.26.pieces_ref = bf16[4,128,512]{2,1,0:T(8,128)(2,1)S(1)} collective-permute-done((bf16[4,128,512]{2,1,0:T(8,128)(2,1)S(1)}, bf16[4,128,512]{2,1,0:T(8,128)(2,1)S(1)}, u32[]{:S(2)}, u32[]{:S(2)}) %collective-permute-start.26) | collective-permute-done | bytes 524320 | tf_op jit(solution)/shard_map/ppermute | solution.py:143
  124.8 2.1 collective-permute-start.32
  128.5 2.4 collective-permute-done.31
  133.7 2.0 collective-permute-start.35
  136.9 3.8 %collective-permute-done.34.pieces_ref = bf16[4,128,512]{2,1,0:T(8,128)(2,1)S(1)} collective-permute-done((bf16[4,128,512]{2,1,0:T(8,128)(2,1)S(1)}, bf16[4,128,512]{2,1,0:T(8,128)(2,1)S(1)}, u32[]{:S(2)}, u32[]{:S(2)}) %collective-permute-start.34) | collective-permute-done | bytes 524320 | tf_op jit(solution)/shard_map/ppermute | solution.py:143
  142.0 6.3 %collective-permute-done.33.pieces_ref = bf16[4,128,512]{2,1,0:T(8,128)(2,1)S(1)} collective-permute-done((bf16[4,128,512]{2,1,0:T(8,128)(2,1)S(1)}, bf16[4,128,512]{2,1,0:T(8,128)(2,1)S(1)}, u32[]{:S(2)}, u32[]{:S(2)}) %collective-permute-start.33) | collective-permute-done | bytes 524320 | tf_op jit(solution)/shard_map/ppermute | solution.py:143
  154.0 2.3 collective-permute-start.39
  156.7 2.2 collective-permute-done.38
  165.4 3.8 %collective-permute-done.41.pieces_ref = bf16[4,128,512]{2,1,0:T(8,128)(2,1)S(1)} collective-permute-done((bf16[4,128,512]{2,1,0:T(8,128)(2,1)S(1)}, bf16[4,128,512]{2,1,0:T(8,128)(2,1)S(1)}, u32[]{:S(2)}, u32[]{:S(2)}) %collective-permute-start.41) | collective-permute-done | bytes 524320 | tf_op jit(solution)/shard_map/ppermute | solution.py:143
  170.4 6.9 %collective-permute-done.40.pieces_ref = bf16[4,128,512]{2,1,0:T(8,128)(2,1)S(1)} collective-permute-done((bf16[4,128,512]{2,1,0:T(8,128)(2,1)S(1)}, bf16[4,128,512]{2,1,0:T(8,128)(2,1)S(1)}, u32[]{:S(2)}, u32[]{:S(2)}) %collective-permute-start.40) | collective-permute-done | bytes 524320 | tf_op jit(solution)/shard_map/ppermute | solution.py:143
  184.6 2.5 collective-permute-done.44
  187.1 2.8 collective-permute-done.45
  195.8 3.8 %collective-permute-done.48.pieces_ref = bf16[4,128,512]{2,1,0:T(8,128)(2,1)S(1)} collective-permute-done((bf16[4,128,512]{2,1,0:T(8,128)(2,1)S(1)}, bf16[4,128,512]{2,1,0:T(8,128)(2,1)S(1)}, u32[]{:S(2)}, u32[]{:S(2)}) %collective-permute-start.48) | collective-permute-done | bytes 524320 | tf_op jit(solution)/shard_map/ppermute | solution.py:143
  200.9 6.5 %collective-permute-done.47.pieces_ref = bf16[4,128,512]{2,1,0:T(8,128)(2,1)S(1)} collective-permute-done((bf16[4,128,512]{2,1,0:T(8,128)(2,1)S(1)}, bf16[4,128,512]{2,1,0:T(8,128)(2,1)S(1)}, u32[]{:S(2)}, u32[]{:S(2)}) %collective-permute-start.47) | collective-permute-done | bytes 524320 | tf_op jit(solution)/shard_map/ppermute | solution.py:143
  216.3 2.5 collective-permute-done.52
  224.4 3.8 %collective-permute-done.55.pieces_ref = bf16[4,128,512]{2,1,0:T(8,128)(2,1)S(1)} collective-permute-done((bf16[4,128,512]{2,1,0:T(8,128)(2,1)S(1)}, bf16[4,128,512]{2,1,0:T(8,128)(2,1)S(1)}, u32[]{:S(2)}, u32[]{:S(2)}) %collective-permute-start.55) | collective-permute-done | bytes 524320 | tf_op jit(solution)/shard_map/ppermute | solution.py:143
  229.5 6.4 %collective-permute-done.54.pieces_ref = bf16[4,128,512]{2,1,0:T(8,128)(2,1)S(1)} collective-permute-done((bf16[4,128,512]{2,1,0:T(8,128)(2,1)S(1)}, bf16[4,128,512]{2,1,0:T(8,128)(2,1)S(1)}, u32[]{:S(2)}, u32[]{:S(2)}) %collective-permute-start.54) | collective-permute-done | bytes 524320 | tf_op jit(solution)/shard_map/ppermute | solution.py:143
  242.6 2.0 collective-permute-done.57
  244.6 2.3 collective-permute-done.59
  252.2 2.2 copy-done.7
  258.0 6.4 %collective-permute-done.61.pieces_ref = bf16[4,128,512]{2,1,0:T(8,128)(2,1)S(1)} collective-permute-done((bf16[4,128,512]{2,1,0:T(8,128)(2,1)S(1)}, bf16[4,128,512]{2,1,0:T(8,128)(2,1)S(1)}, u32[]{:S(2)}, u32[]{:S(2)}) %collective-permute-start.61) | collective-permute-done | bytes 524320 | tf_op jit(solution)/shard_map/ppermute | solution.py:143
  269.9 2.0 collective-permute-start.67
  276.5 2.3 collective-permute-start.69
  282.0 3.7 %collective-permute-done.69.pieces_ref = bf16[4,128,512]{2,1,0:T(8,128)(2,1)S(1)} collective-permute-done((bf16[4,128,512]{2,1,0:T(8,128)(2,1)S(1)}, bf16[4,128,512]{2,1,0:T(8,128)(2,1)S(1)}, u32[]{:S(2)}, u32[]{:S(2)}) %collective-permute-start.69) | collective-permute-done | bytes 524320 | tf_op jit(solution)/shard_map/ppermute | solution.py:143
  287.0 7.1 %collective-permute-done.68.pieces_ref = bf16[4,128,512]{2,1,0:T(8,128)(2,1)S(1)} collective-permute-done((bf16[4,128,512]{2,1,0:T(8,128)(2,1)S(1)}, bf16[4,128,512]{2,1,0:T(8,128)(2,1)S(1)}, u32[]{:S(2)}, u32[]{:S(2)}) %collective-permute-start.68) | collective-permute-done | bytes 524320 | tf_op jit(solution)/shard_map/ppermute | solution.py:143
  302.9 2.8 collective-permute-done.73
  312.1 3.7 %collective-permute-done.76.pieces_ref = bf16[4,128,512]{2,1,0:T(8,128)(2,1)S(1)} collective-permute-done((bf16[4,128,512]{2,1,0:T(8,128)(2,1)S(1)}, bf16[4,128,512]{2,1,0:T(8,128)(2,1)S(1)}, u32[]{:S(2)}, u32[]{:S(2)}) %collective-permute-start.76) | collective-permute-done | bytes 524320 | tf_op jit(solution)/shard_map/ppermute | solution.py:143
  317.0 6.9 %collective-permute-done.75.pieces_ref = bf16[4,128,512]{2,1,0:T(8,128)(2,1)S(1)} collective-permute-done((bf16[4,128,512]{2,1,0:T(8,128)(2,1)S(1)}, bf16[4,128,512]{2,1,0:T(8,128)(2,1)S(1)}, u32[]{:S(2)}, u32[]{:S(2)}) %collective-permute-start.75) | collective-permute-done | bytes 524320 | tf_op jit(solution)/shard_map/ppermute | solution.py:143
  325.2 2.0 finish_product.21
  (209 shorter events, 151.3 us)
Async XLA Ops:
  1.9 7.9 %collective-permute-start = (bf16[128,512]{1,0:T(8,128)(2,1)S(1)}, bf16[128,512]{1,0:T(8,128)(2,1)S(1)}, u32[]{:S(2)}, u32[]{:S(2)}) collective-permute-start(bf16[128,512]{1,0:T(8,128)(2,1)S(1)} %bitcast.136), channel_id=1, source_target_pairs={{0,1},{1,0},{2,3},{3,2},{4,5},{5,4},{6,7},{7,6},{8,9},{9,8},{10,11... | collective-permute-start | bytes 393224 | tf_op jit(solution)/shard_map/ppermute | solution.py:143
  6.8 21.3 %collective-permute-start.6 = (bf16[4,128,512]{2,1,0:T(8,128)(2,1)S(1)}, bf16[4,128,512]{2,1,0:T(8,128)(2,1)S(1)}, u32[]{:S(2)}, u32[]{:S(2)}) collective-permute-start(bf16[4,128,512]{2,1,0:T(8,128)(2,1)S(1)} %bitcast.135), channel_id=1, source_target_pairs={{0,16},{1,17},{2,18},{3,19},{4,20},{5,21},{6,22},{7,23},{8,24},{9,... | collective-permute-start | bytes 1572872 | tf_op jit(solution)/shard_map/ppermute | solution.py:160
  12.3 16.1 %collective-permute-start.4 = (bf16[4,128,512]{2,1,0:T(8,128)(2,1)S(1)}, bf16[4,128,512]{2,1,0:T(8,128)(2,1)S(1)}, u32[]{:S(2)}, u32[]{:S(2)}) collective-permute-start(bf16[4,128,512]{2,1,0:T(8,128)(2,1)S(1)} %pad_maximum_fusion.pieces_ref), channel_id=1, source_target_pairs={{0,4},{1,5},{2,6},{3,7},{4,0},{5,1},{6,2},{7,3},{8,12},{9,13},{10,... | collective-permute-start | bytes 1572872 | tf_op jit(solution)/shard_map/ppermute | solution.py:143
  13.6 16.1 %collective-permute-start.3 = (bf16[4,128,512]{2,1,0:T(8,128)(2,1)S(1)}, bf16[4,128,512]{2,1,0:T(8,128)(2,1)S(1)}, u32[]{:S(2)}, u32[]{:S(2)}) collective-permute-start(bf16[4,128,512]{2,1,0:T(8,128)(2,1)S(1)} %pad_maximum_fusion.pieces_ref), channel_id=1, source_target_pairs={{0,12},{1,13},{2,14},{3,15},{4,8},{5,9},{6,10},{7,11},{8,4},{9,5},... | collective-permute-start | bytes 1572872 | tf_op jit(solution)/shard_map/ppermute | solution.py:143
  15.4 11.4 %collective-permute-start.7 = (f32[1,512]{1,0:T(1,128)S(1)}, f32[1,512]{1,0:T(1,128)S(1)}, u32[]{:S(2)}, u32[]{:S(2)}) collective-permute-start(f32[1,512]{1,0:T(1,128)S(1)} %copy-done.9), channel_id=1, source_target_pairs={{0,16},{1,17},{2,18},{3,19},{4,20},{5,21},{6,22},{7,23},{8,24},{9,... | collective-permute-start | bytes 6152 | tf_op jit(solution)/shard_map/ppermute | solution.py:161
  19.3 11.6 %collective-permute-start.5 = (bf16[4,128,512]{2,1,0:T(8,128)(2,1)S(1)}, bf16[4,128,512]{2,1,0:T(8,128)(2,1)S(1)}, u32[]{:S(2)}, u32[]{:S(2)}) collective-permute-start(bf16[4,128,512]{2,1,0:T(8,128)(2,1)S(1)} %pad_maximum_fusion.pieces_ref), channel_id=1, source_target_pairs={{0,8},{1,9},{2,10},{3,11},{4,12},{5,13},{6,14},{7,15},{8,0},{9,1},... | collective-permute-start | bytes 1572872 | tf_op jit(solution)/shard_map/ppermute | solution.py:143
  32.3 8.1 %collective-permute-start.8 = (bf16[128,512]{1,0:T(8,128)(2,1)S(1)}, bf16[128,512]{1,0:T(8,128)(2,1)S(1)}, u32[]{:S(2)}, u32[]{:S(2)}) collective-permute-start(bf16[128,512]{1,0:T(8,128)(2,1)S(1)} %get-tuple-element.34), channel_id=1, source_target_pairs={{0,112},{1,113},{2,114},{3,115},{4,116},{5,117},{6,118},{7,119},{8... | collective-permute-start | bytes 393224 | tf_op jit(solution)/shard_map/ppermute | solution.py:143
  34.3 8.3 %collective-permute-start.10 = (bf16[128,512]{1,0:T(8,128)(2,1)S(1)}, bf16[128,512]{1,0:T(8,128)(2,1)S(1)}, u32[]{:S(2)}, u32[]{:S(2)}) collective-permute-start(bf16[128,512]{1,0:T(8,128)(2,1)S(1)} %get-tuple-element.34), channel_id=1, source_target_pairs={{0,120},{1,121},{2,122},{3,123},{4,124},{5,125},{6,126},{7,127},{8... | collective-permute-start | bytes 393224 | tf_op jit(solution)/shard_map/ppermute | solution.py:143
  44.2 8.4 %collective-permute-start.13 = (bf16[4,128,512]{2,1,0:T(8,128)(2,1)S(1)}, bf16[4,128,512]{2,1,0:T(8,128)(2,1)S(1)}, u32[]{:S(2)}, u32[]{:S(2)}) collective-permute-start(bf16[4,128,512]{2,1,0:T(8,128)(2,1)S(1)} %pad_maximum_fusion.1.pieces_ref), channel_id=1, source_target_pairs={{0,4},{1,5},{2,6},{3,7},{4,0},{5,1},{6,2},{7,3},{8,12},{9,13},{10,... | collective-permute-start | bytes 1572872 | tf_op jit(solution)/shard_map/ppermute | solution.py:143
  44.9 15.2 %collective-permute-start.12 = (bf16[4,128,512]{2,1,0:T(8,128)(2,1)S(1)}, bf16[4,128,512]{2,1,0:T(8,128)(2,1)S(1)}, u32[]{:S(2)}, u32[]{:S(2)}) collective-permute-start(bf16[4,128,512]{2,1,0:T(8,128)(2,1)S(1)} %pad_maximum_fusion.1.pieces_ref), channel_id=1, source_target_pairs={{0,12},{1,13},{2,14},{3,15},{4,8},{5,9},{6,10},{7,11},{8,4},{9,5},... | collective-permute-start | bytes 1572872 | tf_op jit(solution)/shard_map/ppermute | solution.py:143
  46.8 14.5 %collective-permute-start.14 = (bf16[4,128,512]{2,1,0:T(8,128)(2,1)S(1)}, bf16[4,128,512]{2,1,0:T(8,128)(2,1)S(1)}, u32[]{:S(2)}, u32[]{:S(2)}) collective-permute-start(bf16[4,128,512]{2,1,0:T(8,128)(2,1)S(1)} %pad_maximum_fusion.1.pieces_ref), channel_id=1, source_target_pairs={{0,8},{1,9},{2,10},{3,11},{4,12},{5,13},{6,14},{7,15},{8,0},{9,1},... | collective-permute-start | bytes 1572872 | tf_op jit(solution)/shard_map/ppermute | solution.py:143
  66.1 8.0 %collective-permute-start.17 = (bf16[128,512]{1,0:T(8,128)(2,1)S(1)}, bf16[128,512]{1,0:T(8,128)(2,1)S(1)}, u32[]{:S(2)}, u32[]{:S(2)}) collective-permute-start(bf16[128,512]{1,0:T(8,128)(2,1)S(1)} %get-tuple-element.36), channel_id=1, source_target_pairs={{0,120},{1,121},{2,122},{3,123},{4,124},{5,125},{6,126},{7,127},{8... | collective-permute-start | bytes 393224 | tf_op jit(solution)/shard_map/ppermute | solution.py:143
  67.0 7.9 %collective-permute-start.18 = (bf16[128,512]{1,0:T(8,128)(2,1)S(1)}, bf16[128,512]{1,0:T(8,128)(2,1)S(1)}, u32[]{:S(2)}, u32[]{:S(2)}) collective-permute-start(bf16[128,512]{1,0:T(8,128)(2,1)S(1)} %get-tuple-element.36), channel_id=1, source_target_pairs={{0,124},{1,125},{2,126},{3,127},{4,120},{5,121},{6,122},{7,123},{8... | collective-permute-start | bytes 393224 | tf_op jit(solution)/shard_map/ppermute | solution.py:143
  75.0 8.4 %collective-permute-start.20 = (bf16[4,128,512]{2,1,0:T(8,128)(2,1)S(1)}, bf16[4,128,512]{2,1,0:T(8,128)(2,1)S(1)}, u32[]{:S(2)}, u32[]{:S(2)}) collective-permute-start(bf16[4,128,512]{2,1,0:T(8,128)(2,1)S(1)} %pad_maximum_fusion.2.pieces_ref), channel_id=1, source_target_pairs={{0,4},{1,5},{2,6},{3,7},{4,0},{5,1},{6,2},{7,3},{8,12},{9,13},{10,... | collective-permute-start | bytes 1572872 | tf_op jit(solution)/shard_map/ppermute | solution.py:143
  76.4 14.9 %collective-permute-start.19 = (bf16[4,128,512]{2,1,0:T(8,128)(2,1)S(1)}, bf16[4,128,512]{2,1,0:T(8,128)(2,1)S(1)}, u32[]{:S(2)}, u32[]{:S(2)}) collective-permute-start(bf16[4,128,512]{2,1,0:T(8,128)(2,1)S(1)} %pad_maximum_fusion.2.pieces_ref), channel_id=1, source_target_pairs={{0,12},{1,13},{2,14},{3,15},{4,8},{5,9},{6,10},{7,11},{8,4},{9,5},... | collective-permute-start | bytes 1572872 | tf_op jit(solution)/shard_map/ppermute | solution.py:143
  77.7 14.8 %collective-permute-start.21 = (bf16[4,128,512]{2,1,0:T(8,128)(2,1)S(1)}, bf16[4,128,512]{2,1,0:T(8,128)(2,1)S(1)}, u32[]{:S(2)}, u32[]{:S(2)}) collective-permute-start(bf16[4,128,512]{2,1,0:T(8,128)(2,1)S(1)} %pad_maximum_fusion.2.pieces_ref), channel_id=1, source_target_pairs={{0,8},{1,9},{2,10},{3,11},{4,12},{5,13},{6,14},{7,15},{8,0},{9,1},... | collective-permute-start | bytes 1572872 | tf_op jit(solution)/shard_map/ppermute | solution.py:143
  94.3 8.2 %collective-permute-start.24 = (bf16[128,512]{1,0:T(8,128)(2,1)S(1)}, bf16[128,512]{1,0:T(8,128)(2,1)S(1)}, u32[]{:S(2)}, u32[]{:S(2)}) collective-permute-start(bf16[128,512]{1,0:T(8,128)(2,1)S(1)} %get-tuple-element.38), channel_id=1, source_target_pairs={{0,120},{1,121},{2,122},{3,123},{4,124},{5,125},{6,126},{7,127},{8... | collective-permute-start | bytes 393224 | tf_op jit(solution)/shard_map/ppermute | solution.py:143
  95.4 7.9 %collective-permute-start.25 = (bf16[128,512]{1,0:T(8,128)(2,1)S(1)}, bf16[128,512]{1,0:T(8,128)(2,1)S(1)}, u32[]{:S(2)}, u32[]{:S(2)}) collective-permute-start(bf16[128,512]{1,0:T(8,128)(2,1)S(1)} %get-tuple-element.38), channel_id=1, source_target_pairs={{0,124},{1,125},{2,126},{3,127},{4,120},{5,121},{6,122},{7,123},{8... | collective-permute-start | bytes 393224 | tf_op jit(solution)/shard_map/ppermute | solution.py:143
  103.4 8.8 %collective-permute-start.27 = (bf16[4,128,512]{2,1,0:T(8,128)(2,1)S(1)}, bf16[4,128,512]{2,1,0:T(8,128)(2,1)S(1)}, u32[]{:S(2)}, u32[]{:S(2)}) collective-permute-start(bf16[4,128,512]{2,1,0:T(8,128)(2,1)S(1)} %pad_maximum_fusion.3.pieces_ref), channel_id=1, source_target_pairs={{0,4},{1,5},{2,6},{3,7},{4,0},{5,1},{6,2},{7,3},{8,12},{9,13},{10,... | collective-permute-start | bytes 1572872 | tf_op jit(solution)/shard_map/ppermute | solution.py:143
  104.8 15.0 %collective-permute-start.26 = (bf16[4,128,512]{2,1,0:T(8,128)(2,1)S(1)}, bf16[4,128,512]{2,1,0:T(8,128)(2,1)S(1)}, u32[]{:S(2)}, u32[]{:S(2)}) collective-permute-start(bf16[4,128,512]{2,1,0:T(8,128)(2,1)S(1)} %pad_maximum_fusion.3.pieces_ref), channel_id=1, source_target_pairs={{0,12},{1,13},{2,14},{3,15},{4,8},{5,9},{6,10},{7,11},{8,4},{9,5},... | collective-permute-start | bytes 1572872 | tf_op jit(solution)/shard_map/ppermute | solution.py:143
  105.9 15.1 %collective-permute-start.28 = (bf16[4,128,512]{2,1,0:T(8,128)(2,1)S(1)}, bf16[4,128,512]{2,1,0:T(8,128)(2,1)S(1)}, u32[]{:S(2)}, u32[]{:S(2)}) collective-permute-start(bf16[4,128,512]{2,1,0:T(8,128)(2,1)S(1)} %pad_maximum_fusion.3.pieces_ref), channel_id=1, source_target_pairs={{0,8},{1,9},{2,10},{3,11},{4,12},{5,13},{6,14},{7,15},{8,0},{9,1},... | collective-permute-start | bytes 1572872 | tf_op jit(solution)/shard_map/ppermute | solution.py:143
  132.3 8.4 %collective-permute-start.34 = (bf16[4,128,512]{2,1,0:T(8,128)(2,1)S(1)}, bf16[4,128,512]{2,1,0:T(8,128)(2,1)S(1)}, u32[]{:S(2)}, u32[]{:S(2)}) collective-permute-start(bf16[4,128,512]{2,1,0:T(8,128)(2,1)S(1)} %pad_maximum_fusion.4.pieces_ref), channel_id=1, source_target_pairs={{0,4},{1,5},{2,6},{3,7},{4,0},{5,1},{6,2},{7,3},{8,12},{9,13},{10,... | collective-permute-start | bytes 1572872 | tf_op jit(solution)/shard_map/ppermute | solution.py:143
  133.1 15.1 %collective-permute-start.33 = (bf16[4,128,512]{2,1,0:T(8,128)(2,1)S(1)}, bf16[4,128,512]{2,1,0:T(8,128)(2,1)S(1)}, u32[]{:S(2)}, u32[]{:S(2)}) collective-permute-start(bf16[4,128,512]{2,1,0:T(8,128)(2,1)S(1)} %pad_maximum_fusion.4.pieces_ref), channel_id=1, source_target_pairs={{0,12},{1,13},{2,14},{3,15},{4,8},{5,9},{6,10},{7,11},{8,4},{9,5},... | collective-permute-start | bytes 1572872 | tf_op jit(solution)/shard_map/ppermute | solution.py:143
  133.7 15.9 %collective-permute-start.35 = (bf16[4,128,512]{2,1,0:T(8,128)(2,1)S(1)}, bf16[4,128,512]{2,1,0:T(8,128)(2,1)S(1)}, u32[]{:S(2)}, u32[]{:S(2)}) collective-permute-start(bf16[4,128,512]{2,1,0:T(8,128)(2,1)S(1)} %pad_maximum_fusion.4.pieces_ref), channel_id=1, source_target_pairs={{0,8},{1,9},{2,10},{3,11},{4,12},{5,13},{6,14},{7,15},{8,0},{9,1},... | collective-permute-start | bytes 1572872 | tf_op jit(solution)/shard_map/ppermute | solution.py:143
  160.8 8.4 %collective-permute-start.41 = (bf16[4,128,512]{2,1,0:T(8,128)(2,1)S(1)}, bf16[4,128,512]{2,1,0:T(8,128)(2,1)S(1)}, u32[]{:S(2)}, u32[]{:S(2)}) collective-permute-start(bf16[4,128,512]{2,1,0:T(8,128)(2,1)S(1)} %pad_maximum_fusion.5.pieces_ref), channel_id=1, source_target_pairs={{0,4},{1,5},{2,6},{3,7},{4,0},{5,1},{6,2},{7,3},{8,12},{9,13},{10,... | collective-permute-start | bytes 1572872 | tf_op jit(solution)/shard_map/ppermute | solution.py:143
  162.2 15.2 %collective-permute-start.40 = (bf16[4,128,512]{2,1,0:T(8,128)(2,1)S(1)}, bf16[4,128,512]{2,1,0:T(8,128)(2,1)S(1)}, u32[]{:S(2)}, u32[]{:S(2)}) collective-permute-start(bf16[4,128,512]{2,1,0:T(8,128)(2,1)S(1)} %pad_maximum_fusion.5.pieces_ref), channel_id=1, source_target_pairs={{0,12},{1,13},{2,14},{3,15},{4,8},{5,9},{6,10},{7,11},{8,4},{9,5},... | collective-permute-start | bytes 1572872 | tf_op jit(solution)/shard_map/ppermute | solution.py:143
  163.6 15.0 %collective-permute-start.42 = (bf16[4,128,512]{2,1,0:T(8,128)(2,1)S(1)}, bf16[4,128,512]{2,1,0:T(8,128)(2,1)S(1)}, u32[]{:S(2)}, u32[]{:S(2)}) collective-permute-start(bf16[4,128,512]{2,1,0:T(8,128)(2,1)S(1)} %pad_maximum_fusion.5.pieces_ref), channel_id=1, source_target_pairs={{0,8},{1,9},{2,10},{3,11},{4,12},{5,13},{6,14},{7,15},{8,0},{9,1},... | collective-permute-start | bytes 1572872 | tf_op jit(solution)/shard_map/ppermute | solution.py:143
  182.3 7.6 %collective-permute-start.45 = (bf16[128,512]{1,0:T(8,128)(2,1)S(1)}, bf16[128,512]{1,0:T(8,128)(2,1)S(1)}, u32[]{:S(2)}, u32[]{:S(2)}) collective-permute-start(bf16[128,512]{1,0:T(8,128)(2,1)S(1)} %get-tuple-element.44), channel_id=1, source_target_pairs={{0,120},{1,121},{2,122},{3,123},{4,124},{5,125},{6,126},{7,127},{8... | collective-permute-start | bytes 393224 | tf_op jit(solution)/shard_map/ppermute | solution.py:143
  183.3 7.9 %collective-permute-start.46 = (bf16[128,512]{1,0:T(8,128)(2,1)S(1)}, bf16[128,512]{1,0:T(8,128)(2,1)S(1)}, u32[]{:S(2)}, u32[]{:S(2)}) collective-permute-start(bf16[128,512]{1,0:T(8,128)(2,1)S(1)} %get-tuple-element.44), channel_id=1, source_target_pairs={{0,124},{1,125},{2,126},{3,127},{4,120},{5,121},{6,122},{7,123},{8... | collective-permute-start | bytes 393224 | tf_op jit(solution)/shard_map/ppermute | solution.py:143
  191.3 8.4 %collective-permute-start.48 = (bf16[4,128,512]{2,1,0:T(8,128)(2,1)S(1)}, bf16[4,128,512]{2,1,0:T(8,128)(2,1)S(1)}, u32[]{:S(2)}, u32[]{:S(2)}) collective-permute-start(bf16[4,128,512]{2,1,0:T(8,128)(2,1)S(1)} %pad_maximum_fusion.6.pieces_ref), channel_id=1, source_target_pairs={{0,4},{1,5},{2,6},{3,7},{4,0},{5,1},{6,2},{7,3},{8,12},{9,13},{10,... | collective-permute-start | bytes 1572872 | tf_op jit(solution)/shard_map/ppermute | solution.py:143
  192.6 14.9 %collective-permute-start.47 = (bf16[4,128,512]{2,1,0:T(8,128)(2,1)S(1)}, bf16[4,128,512]{2,1,0:T(8,128)(2,1)S(1)}, u32[]{:S(2)}, u32[]{:S(2)}) collective-permute-start(bf16[4,128,512]{2,1,0:T(8,128)(2,1)S(1)} %pad_maximum_fusion.6.pieces_ref), channel_id=1, source_target_pairs={{0,12},{1,13},{2,14},{3,15},{4,8},{5,9},{6,10},{7,11},{8,4},{9,5},... | collective-permute-start | bytes 1572872 | tf_op jit(solution)/shard_map/ppermute | solution.py:143
  193.9 14.8 %collective-permute-start.49 = (bf16[4,128,512]{2,1,0:T(8,128)(2,1)S(1)}, bf16[4,128,512]{2,1,0:T(8,128)(2,1)S(1)}, u32[]{:S(2)}, u32[]{:S(2)}) collective-permute-start(bf16[4,128,512]{2,1,0:T(8,128)(2,1)S(1)} %pad_maximum_fusion.6.pieces_ref), channel_id=1, source_target_pairs={{0,8},{1,9},{2,10},{3,11},{4,12},{5,13},{6,14},{7,15},{8,0},{9,1},... | collective-permute-start | bytes 1572872 | tf_op jit(solution)/shard_map/ppermute | solution.py:143
  210.7 8.1 %collective-permute-start.52 = (bf16[128,512]{1,0:T(8,128)(2,1)S(1)}, bf16[128,512]{1,0:T(8,128)(2,1)S(1)}, u32[]{:S(2)}, u32[]{:S(2)}) collective-permute-start(bf16[128,512]{1,0:T(8,128)(2,1)S(1)} %get-tuple-element.46), channel_id=1, source_target_pairs={{0,120},{1,121},{2,122},{3,123},{4,124},{5,125},{6,126},{7,127},{8... | collective-permute-start | bytes 393224 | tf_op jit(solution)/shard_map/ppermute | solution.py:143
  211.9 7.9 %collective-permute-start.53 = (bf16[128,512]{1,0:T(8,128)(2,1)S(1)}, bf16[128,512]{1,0:T(8,128)(2,1)S(1)}, u32[]{:S(2)}, u32[]{:S(2)}) collective-permute-start(bf16[128,512]{1,0:T(8,128)(2,1)S(1)} %get-tuple-element.46), channel_id=1, source_target_pairs={{0,124},{1,125},{2,126},{3,127},{4,120},{5,121},{6,122},{7,123},{8... | collective-permute-start | bytes 393224 | tf_op jit(solution)/shard_map/ppermute | solution.py:143
  219.8 8.4 %collective-permute-start.55 = (bf16[4,128,512]{2,1,0:T(8,128)(2,1)S(1)}, bf16[4,128,512]{2,1,0:T(8,128)(2,1)S(1)}, u32[]{:S(2)}, u32[]{:S(2)}) collective-permute-start(bf16[4,128,512]{2,1,0:T(8,128)(2,1)S(1)} %pad_maximum_fusion.7.pieces_ref), channel_id=1, source_target_pairs={{0,4},{1,5},{2,6},{3,7},{4,0},{5,1},{6,2},{7,3},{8,12},{9,13},{10,... | collective-permute-start | bytes 1572872 | tf_op jit(solution)/shard_map/ppermute | solution.py:143
  220.9 14.9 %collective-permute-start.54 = (bf16[4,128,512]{2,1,0:T(8,128)(2,1)S(1)}, bf16[4,128,512]{2,1,0:T(8,128)(2,1)S(1)}, u32[]{:S(2)}, u32[]{:S(2)}) collective-permute-start(bf16[4,128,512]{2,1,0:T(8,128)(2,1)S(1)} %pad_maximum_fusion.7.pieces_ref), channel_id=1, source_target_pairs={{0,12},{1,13},{2,14},{3,15},{4,8},{5,9},{6,10},{7,11},{8,4},{9,5},... | collective-permute-start | bytes 1572872 | tf_op jit(solution)/shard_map/ppermute | solution.py:143
  222.3 14.8 %collective-permute-start.56 = (bf16[4,128,512]{2,1,0:T(8,128)(2,1)S(1)}, bf16[4,128,512]{2,1,0:T(8,128)(2,1)S(1)}, u32[]{:S(2)}, u32[]{:S(2)}) collective-permute-start(bf16[4,128,512]{2,1,0:T(8,128)(2,1)S(1)} %pad_maximum_fusion.7.pieces_ref), channel_id=1, source_target_pairs={{0,8},{1,9},{2,10},{3,11},{4,12},{5,13},{6,14},{7,15},{8,0},{9,1},... | collective-permute-start | bytes 1572872 | tf_op jit(solution)/shard_map/ppermute | solution.py:143
  248.4 8.4 %collective-permute-start.62 = (bf16[4,128,512]{2,1,0:T(8,128)(2,1)S(1)}, bf16[4,128,512]{2,1,0:T(8,128)(2,1)S(1)}, u32[]{:S(2)}, u32[]{:S(2)}) collective-permute-start(bf16[4,128,512]{2,1,0:T(8,128)(2,1)S(1)} %pad_maximum_fusion.8.pieces_ref), channel_id=1, source_target_pairs={{0,4},{1,5},{2,6},{3,7},{4,0},{5,1},{6,2},{7,3},{8,12},{9,13},{10,... | collective-permute-start | bytes 1572872 | tf_op jit(solution)/shard_map/ppermute | solution.py:143
  249.4 15.0 %collective-permute-start.61 = (bf16[4,128,512]{2,1,0:T(8,128)(2,1)S(1)}, bf16[4,128,512]{2,1,0:T(8,128)(2,1)S(1)}, u32[]{:S(2)}, u32[]{:S(2)}) collective-permute-start(bf16[4,128,512]{2,1,0:T(8,128)(2,1)S(1)} %pad_maximum_fusion.8.pieces_ref), channel_id=1, source_target_pairs={{0,12},{1,13},{2,14},{3,15},{4,8},{5,9},{6,10},{7,11},{8,4},{9,5},... | collective-permute-start | bytes 1572872 | tf_op jit(solution)/shard_map/ppermute | solution.py:143
  250.9 14.8 %collective-permute-start.63 = (bf16[4,128,512]{2,1,0:T(8,128)(2,1)S(1)}, bf16[4,128,512]{2,1,0:T(8,128)(2,1)S(1)}, u32[]{:S(2)}, u32[]{:S(2)}) collective-permute-start(bf16[4,128,512]{2,1,0:T(8,128)(2,1)S(1)} %pad_maximum_fusion.8.pieces_ref), channel_id=1, source_target_pairs={{0,8},{1,9},{2,10},{3,11},{4,12},{5,13},{6,14},{7,15},{8,0},{9,1},... | collective-permute-start | bytes 1572872 | tf_op jit(solution)/shard_map/ppermute | solution.py:143
  276.5 9.2 %collective-permute-start.69 = (bf16[4,128,512]{2,1,0:T(8,128)(2,1)S(1)}, bf16[4,128,512]{2,1,0:T(8,128)(2,1)S(1)}, u32[]{:S(2)}, u32[]{:S(2)}) collective-permute-start(bf16[4,128,512]{2,1,0:T(8,128)(2,1)S(1)} %pad_maximum_fusion.9.pieces_ref), channel_id=1, source_target_pairs={{0,4},{1,5},{2,6},{3,7},{4,0},{5,1},{6,2},{7,3},{8,12},{9,13},{10,... | collective-permute-start | bytes 1572872 | tf_op jit(solution)/shard_map/ppermute | solution.py:143
  278.9 15.2 %collective-permute-start.68 = (bf16[4,128,512]{2,1,0:T(8,128)(2,1)S(1)}, bf16[4,128,512]{2,1,0:T(8,128)(2,1)S(1)}, u32[]{:S(2)}, u32[]{:S(2)}) collective-permute-start(bf16[4,128,512]{2,1,0:T(8,128)(2,1)S(1)} %pad_maximum_fusion.9.pieces_ref), channel_id=1, source_target_pairs={{0,12},{1,13},{2,14},{3,15},{4,8},{5,9},{6,10},{7,11},{8,4},{9,5},... | collective-permute-start | bytes 1572872 | tf_op jit(solution)/shard_map/ppermute | solution.py:143
  280.1 15.3 %collective-permute-start.70 = (bf16[4,128,512]{2,1,0:T(8,128)(2,1)S(1)}, bf16[4,128,512]{2,1,0:T(8,128)(2,1)S(1)}, u32[]{:S(2)}, u32[]{:S(2)}) collective-permute-start(bf16[4,128,512]{2,1,0:T(8,128)(2,1)S(1)} %pad_maximum_fusion.9.pieces_ref), channel_id=1, source_target_pairs={{0,8},{1,9},{2,10},{3,11},{4,12},{5,13},{6,14},{7,15},{8,0},{9,1},... | collective-permute-start | bytes 1572872 | tf_op jit(solution)/shard_map/ppermute | solution.py:143
  298.2 7.5 %collective-permute-start.73 = (bf16[128,512]{1,0:T(8,128)(2,1)S(1)}, bf16[128,512]{1,0:T(8,128)(2,1)S(1)}, u32[]{:S(2)}, u32[]{:S(2)}) collective-permute-start(bf16[128,512]{1,0:T(8,128)(2,1)S(1)} %get-tuple-element.52), channel_id=1, source_target_pairs={{0,120},{1,121},{2,122},{3,123},{4,124},{5,125},{6,126},{7,127},{8... | collective-permute-start | bytes 393224 | tf_op jit(solution)/shard_map/ppermute | solution.py:143
  299.3 7.7 %collective-permute-start.74 = (bf16[128,512]{1,0:T(8,128)(2,1)S(1)}, bf16[128,512]{1,0:T(8,128)(2,1)S(1)}, u32[]{:S(2)}, u32[]{:S(2)}) collective-permute-start(bf16[128,512]{1,0:T(8,128)(2,1)S(1)} %get-tuple-element.52), channel_id=1, source_target_pairs={{0,124},{1,125},{2,126},{3,127},{4,120},{5,121},{6,122},{7,123},{8... | collective-permute-start | bytes 393224 | tf_op jit(solution)/shard_map/ppermute | solution.py:143
  307.1 8.7 %collective-permute-start.76 = (bf16[4,128,512]{2,1,0:T(8,128)(2,1)S(1)}, bf16[4,128,512]{2,1,0:T(8,128)(2,1)S(1)}, u32[]{:S(2)}, u32[]{:S(2)}) collective-permute-start(bf16[4,128,512]{2,1,0:T(8,128)(2,1)S(1)} %pad_maximum_fusion.10.pieces_ref), channel_id=1, source_target_pairs={{0,4},{1,5},{2,6},{3,7},{4,0},{5,1},{6,2},{7,3},{8,12},{9,13},{10,... | collective-permute-start | bytes 1572872 | tf_op jit(solution)/shard_map/ppermute | solution.py:143
  308.9 15.0 %collective-permute-start.75 = (bf16[4,128,512]{2,1,0:T(8,128)(2,1)S(1)}, bf16[4,128,512]{2,1,0:T(8,128)(2,1)S(1)}, u32[]{:S(2)}, u32[]{:S(2)}) collective-permute-start(bf16[4,128,512]{2,1,0:T(8,128)(2,1)S(1)} %pad_maximum_fusion.10.pieces_ref), channel_id=1, source_target_pairs={{0,12},{1,13},{2,14},{3,15},{4,8},{5,9},{6,10},{7,11},{8,4},{9,5},... | collective-permute-start | bytes 1572872 | tf_op jit(solution)/shard_map/ppermute | solution.py:143
  310.4 14.8 %collective-permute-start.77 = (bf16[4,128,512]{2,1,0:T(8,128)(2,1)S(1)}, bf16[4,128,512]{2,1,0:T(8,128)(2,1)S(1)}, u32[]{:S(2)}, u32[]{:S(2)}) collective-permute-start(bf16[4,128,512]{2,1,0:T(8,128)(2,1)S(1)} %pad_maximum_fusion.10.pieces_ref), channel_id=1, source_target_pairs={{0,8},{1,9},{2,10},{3,11},{4,12},{5,13},{6,14},{7,15},{8,0},{9,1},... | collective-permute-start | bytes 1572872 | tf_op jit(solution)/shard_map/ppermute | solution.py:143
  (40 other events, 1032.1 us)
